TPU v7x, 32 devices: a whole 2x2x4 slice. The times are simulated.
32 devices in a mesh: win: 16 (over z, y, core), tp: 2 (over x).
Axes of the slice: x: 2, y: 2, z: 4, core: 2. Of those that a mesh axis runs over, the one named last changes fastest.
Arguments:
- tokens: bfloat16 [16, 56, 28, 384], P('win', 'tp'), may hold values from -6 to 6
- crop_ids: int32 [16, 56, 28], P('win'), may hold values from 0 to 5, as said below
- cotangent: bfloat16 [16, 56, 28, 384], P('win', 'tp'), may hold values from -6 to 6
- norm_gain: float32 [2, 2, 384], replicated, may hold values from 0.25 to 1.75
- norm_bias: float32 [2, 2, 384], replicated, may hold values from -1.75 to 1.75
- qkv_weight: bfloat16 [2, 384, 3, 384], P(None, None, None, 'tp'), may hold values from -0.3125 to 0.3125
- qv_bias: float32 [2, 2, 384], P(None, None, 'tp'), may hold values from -1.75 to 1.75
- proj_weight: bfloat16 [2, 384, 384], P(None, 'tp'), may hold values from -0.875 to 0.875
- proj_bias: float32 [2, 384], replicated, may hold values from -1.75 to 1.75
- fc1_weight: bfloat16 [2, 384, 1536], P(None, None, 'tp'), may hold values from -0.3125 to 0.3125
- fc1_bias: float32 [2, 1536], P(None, 'tp'), may hold values from -1.75 to 1.75
- fc2_weight: bfloat16 [2, 1536, 384], P(None, 'tp'), may hold values from -0.15625 to 0.15625
- fc2_bias: float32 [2, 384], replicated, may hold values from -1.75 to 1.75
- pos_table: float32 [2, 169, 12], P(None, None, 'tp'), may hold values from -6 to 6
Outputs:
- layer_out: bfloat16 [16, 56, 28, 384], P('win', 'tp')
- grad_tokens: float32 [16, 56, 28, 384], P('win', 'tp')
- grad_norm_gain: float32 [2, 2, 384], replicated
- grad_norm_bias: float32 [2, 2, 384], replicated
- grad_qkv_weight: float32 [2, 384, 3, 384], P(None, None, None, 'tp')
- grad_qv_bias: float32 [2, 2, 384], P(None, None, 'tp')
- grad_proj_weight: float32 [2, 384, 384], P(None, 'tp')
- grad_proj_bias: float32 [2, 384], replicated
- grad_fc1_weight: float32 [2, 384, 1536], P(None, None, 'tp')
- grad_fc1_bias: float32 [2, 1536], P(None, 'tp')
- grad_fc2_weight: float32 [2, 1536, 384], P(None, 'tp')
- grad_fc2_bias: float32 [2, 384], replicated
- grad_pos_table: float32 [2, 169, 12], P(None, None, 'tp')
Inputs may be any that keep to these rules, and one draw needn't show every extreme that they name: `crop_ids`: in each canvas the ids form a grid of three bands of rows by two bands of columns, numbered band of rows * 2 + band of columns; the middle band of rows holds rows 14 to 41 and more; every id occurs in every canvas.
All inputs are finite; a program needn't handle non-finite values.
Results may differ from a plain program's by a relative error of at most 0.024.
Values may be sent and summed in bfloat16 or wider, within the bound.
No kernel may reach another device: no remote copies, remote signals or barrier semaphores. Data moves between devices by JAX's collectives and lax.ppermute only.
A program may use at most 192 MiB of HBM per device.

v0:
```python
from functools import partial

import jax
import jax.numpy as jnp
from jax import lax
from jax.sharding import PartitionSpec as P

C = 384
WIN = 7
SHIFT = 3
LAYERS = 2
HD = 32


negative_fill = -1000000000.0
norm_eps = 1e-05


def layer_norm(values, gain_row, offset):
    average = jnp.mean(values, -1, keepdims=True)
    centred = values - average
    spread = jnp.mean(centred * centred, -1, keepdims=True)
    factor = lax.rsqrt(spread + norm_eps)
    scaled = centred * factor
    return (scaled * gain_row + offset, scaled, factor)


def norm_back(grad_rows, scaled, factor, gain_row):
    dscaled = grad_rows * gain_row
    return factor * (
        dscaled
        - jnp.mean(dscaled, -1, keepdims=True)
        - scaled * jnp.mean(dscaled * scaled, -1, keepdims=True)
    )


def to_windows(canvas):
    height, across = (canvas.shape[0], canvas.shape[1])
    blocks = canvas.reshape(height // WIN, WIN, across // WIN, WIN, -1)
    return blocks.transpose(0, 2, 1, 3, 4).reshape(-1, WIN * WIN, canvas.shape[-1])


def from_windows(blocks, height, across):
    tiles = blocks.reshape(height // WIN, across // WIN, WIN, WIN, -1)
    return tiles.transpose(0, 2, 1, 3, 4).reshape(height, across, -1)


def table_map():
    places = jnp.arange(WIN * WIN, dtype=jnp.int32)
    row_of = places // WIN
    col_of = places % WIN
    index = (row_of[:, None] - row_of[None, :] + WIN - 1) * (2 * WIN - 1) + (
        col_of[:, None] - col_of[None, :] + WIN - 1
    )
    offsets_all = jnp.arange((2 * WIN - 1) ** 2, dtype=jnp.int32)
    return (index.reshape(-1)[:, None] == offsets_all[None, :]).astype(jnp.float32)


def window_mask(crop_grid, shifted):
    height, across = crop_grid.shape
    amount = SHIFT if shifted else 0
    rolled = jnp.roll(crop_grid, (-amount, -amount), (0, 1))
    if shifted:
        row_ids = jnp.arange(height, dtype=jnp.int32)
        col_ids = jnp.arange(across, dtype=jnp.int32)
        row_zone = (row_ids >= height - WIN).astype(jnp.int32) + (row_ids >= height - SHIFT).astype(
            jnp.int32
        )
        col_zone = (col_ids >= across - WIN).astype(jnp.int32) + (col_ids >= across - SHIFT).astype(
            jnp.int32
        )
        rolled = rolled * 9 + row_zone[:, None] * 3 + col_zone[None, :]
    labels = to_windows(rolled[:, :, None])[:, :, 0]
    return labels[:, :, None] == labels[:, None, :]


def gather_grad(grad_rows):
    return lax.all_gather(grad_rows.astype(jnp.bfloat16), "tp", axis=1, tiled=True)[0]


def scatter_grad(partial_rows):
    return lax.psum_scatter(
        partial_rows.astype(jnp.bfloat16), "tp", scatter_dimension=1, tiled=True
    ).astype(jnp.float32)


def layer_forward(states, crop_grid, weights, shifted, onehot):
    gain_pair, offsets, qkv_w, qv_b, proj_w, proj_b, fc1_w, fc1_b, fc2_w, fc2_b, rel_table = weights
    amount = SHIFT if shifted else 0
    local_cols = qkv_w.shape[2]
    heads_here = local_cols // HD
    query_scale = HD ** (-0.5)
    normed, scaled_one, factor_one = layer_norm(states, gain_pair[0], offsets[0])
    normed_low = normed.astype(jnp.bfloat16)
    gathered = lax.all_gather(normed_low, "tp", axis=1, tiled=True)[0]
    height, across = (gathered.shape[0], gathered.shape[1])
    windows = to_windows(jnp.roll(gathered, (-amount, -amount), (0, 1)))
    count = windows.shape[0]
    flat_rows = windows.reshape(-1, C)
    projected = jnp.dot(
        flat_rows, qkv_w.reshape(C, 3 * local_cols), preferred_element_type=jnp.float32
    )
    projected = projected.reshape(count, WIN * WIN, 3, local_cols)
    queries = (
        ((projected[:, :, 0] + qv_b[0]) * query_scale)
        .astype(jnp.bfloat16)
        .reshape(count, WIN * WIN, heads_here, HD)
    )
    key_rows = projected[:, :, 1].astype(jnp.bfloat16).reshape(count, WIN * WIN, heads_here, HD)
    value_rows = (
        (projected[:, :, 2] + qv_b[1])
        .astype(jnp.bfloat16)
        .reshape(count, WIN * WIN, heads_here, HD)
    )
    bias_map = (
        jnp.dot(onehot, rel_table, precision=lax.Precision.HIGHEST)
        .reshape(WIN * WIN, WIN * WIN, heads_here)
        .transpose(2, 0, 1)
    )
    allowed = window_mask(crop_grid, shifted)
    scores = jnp.einsum("wqhd,wkhd->whqk", queries, key_rows, preferred_element_type=jnp.float32)
    scores = jnp.where(allowed[:, None], scores + bias_map[None], negative_fill)
    row_peak = jnp.max(scores, -1, keepdims=True)
    exp_scores = jnp.exp(scores - row_peak)
    attn_probs = exp_scores / jnp.sum(exp_scores, -1, keepdims=True)
    mixed_heads = jnp.einsum(
        "whqk,wkhd->wqhd",
        attn_probs.astype(jnp.bfloat16),
        value_rows,
        preferred_element_type=jnp.float32,
    )
    mixed_low = mixed_heads.reshape(-1, local_cols).astype(jnp.bfloat16)
    partial_rows = jnp.dot(mixed_low, proj_w, preferred_element_type=jnp.float32)
    partial_canvas = jnp.roll(
        from_windows(partial_rows.reshape(count, WIN * WIN, C), height, across),
        (amount, amount),
        (0, 1),
    )
    branch = lax.psum_scatter(partial_canvas[None], "tp", scatter_dimension=1, tiled=True) + proj_b
    hidden_rows = states + branch
    normed_two, scaled_two, factor_two = layer_norm(hidden_rows, gain_pair[1], offsets[1])
    gathered_two = lax.all_gather(normed_two.astype(jnp.bfloat16), "tp", axis=1, tiled=True)
    flat_two = gathered_two.reshape(-1, C)
    upper_rows = jnp.dot(flat_two, fc1_w, preferred_element_type=jnp.float32) + fc1_b
    active = jax.nn.gelu(upper_rows, approximate=False).astype(jnp.bfloat16)
    partial_two = jnp.dot(active, fc2_w, preferred_element_type=jnp.float32).reshape(
        gathered_two.shape
    )
    result = (
        lax.psum_scatter(
            partial_two.astype(jnp.bfloat16), "tp", scatter_dimension=1, tiled=True
        ).astype(jnp.float32)
        + fc2_b
    )
    stored = (
        scaled_one,
        factor_one,
        flat_rows,
        queries,
        key_rows,
        value_rows,
        attn_probs,
        mixed_low,
        scaled_two,
        factor_two,
        flat_two,
        upper_rows,
        active,
    )
    return (hidden_rows + result, stored)


def layer_backward(grad_rows, stored, weights, shifted, onehot):
    gain_pair, offsets, qkv_w, qv_b, proj_w, proj_b, fc1_w, fc1_b, fc2_w, fc2_b, rel_table = weights
    (
        scaled_one,
        factor_one,
        flat_rows,
        queries,
        key_rows,
        value_rows,
        attn_probs,
        mixed_low,
        scaled_two,
        factor_two,
        flat_two,
        upper_rows,
        active,
    ) = stored
    amount = SHIFT if shifted else 0
    local_cols = qkv_w.shape[2]
    heads_here = local_cols // HD
    count = queries.shape[0]
    query_scale = HD ** (-0.5)
    grad_result = grad_rows.astype(jnp.bfloat16)
    grad_fc2_b = jnp.sum(grad_result.astype(jnp.float32), (0, 1, 2))
    gathered = gather_grad(grad_rows)
    height, across = (gathered.shape[0], gathered.shape[1])
    flat_grad = gathered.reshape(-1, C)
    grad_fc2_w = jnp.einsum("tf,tc->fc", active, flat_grad, preferred_element_type=jnp.float32)
    grad_active = jnp.einsum("tc,fc->tf", flat_grad, fc2_w, preferred_element_type=jnp.float32)
    gelu_pull = jax.vjp(partial(jax.nn.gelu, approximate=False), upper_rows)[1]
    grad_upper = gelu_pull(grad_active)[0].astype(jnp.bfloat16)
    grad_fc1_b = jnp.sum(grad_upper.astype(jnp.float32), 0)
    grad_fc1_w = jnp.einsum("tc,tf->cf", flat_two, grad_upper, preferred_element_type=jnp.float32)
    grad_normed_two = jnp.einsum("tf,cf->tc", grad_upper, fc1_w, preferred_element_type=jnp.float32)
    grad_normed_two = scatter_grad(grad_normed_two.reshape(1, height, across, C))
    grad_gain_two = jnp.sum(grad_normed_two * scaled_two, (0, 1, 2))
    grad_offset_two = jnp.sum(grad_normed_two, (0, 1, 2))
    grad_hidden = grad_rows + norm_back(grad_normed_two, scaled_two, factor_two, gain_pair[1])
    grad_branch = grad_hidden.astype(jnp.bfloat16)
    grad_proj_b = jnp.sum(grad_branch.astype(jnp.float32), (0, 1, 2))
    gathered_two = gather_grad(grad_hidden)
    windows_grad = to_windows(jnp.roll(gathered_two, (-amount, -amount), (0, 1))).reshape(-1, C)
    grad_proj_w = jnp.einsum(
        "tk,tc->kc", mixed_low, windows_grad, preferred_element_type=jnp.float32
    )
    grad_mixed = jnp.einsum("tc,kc->tk", windows_grad, proj_w, preferred_element_type=jnp.float32)
    grad_mixed = grad_mixed.astype(jnp.bfloat16).reshape(count, WIN * WIN, heads_here, HD)
    grad_probs = jnp.einsum(
        "wqhd,wkhd->whqk", grad_mixed, value_rows, preferred_element_type=jnp.float32
    )
    grad_values = jnp.einsum(
        "whqk,wqhd->wkhd",
        attn_probs.astype(jnp.bfloat16),
        grad_mixed,
        preferred_element_type=jnp.float32,
    ).astype(jnp.bfloat16)
    grad_scores = attn_probs * (grad_probs - jnp.sum(grad_probs * attn_probs, -1, keepdims=True))
    grad_bias = jnp.sum(grad_scores, 0).transpose(1, 2, 0).reshape(-1, heads_here)
    grad_table = jnp.einsum("pt,ph->th", onehot, grad_bias, precision=lax.Precision.HIGHEST)
    scores_low = grad_scores.astype(jnp.bfloat16)
    grad_queries = jnp.einsum(
        "whqk,wkhd->wqhd", scores_low, key_rows, preferred_element_type=jnp.float32
    ).astype(jnp.bfloat16)
    grad_keys = jnp.einsum(
        "whqk,wqhd->wkhd", scores_low, queries, preferred_element_type=jnp.float32
    ).astype(jnp.bfloat16)
    grad_triple = jnp.stack(
        [
            grad_queries.reshape(-1, local_cols),
            grad_keys.reshape(-1, local_cols),
            grad_values.reshape(-1, local_cols),
        ],
        1,
    )
    column_scale = jnp.array([query_scale, 1.0, 1.0], jnp.float32)[None, :, None]
    grad_qkv_w = (
        jnp.einsum("tc,tjk->cjk", flat_rows, grad_triple, preferred_element_type=jnp.float32)
        * column_scale
    )
    grad_qv_b = jnp.stack(
        [
            jnp.sum(grad_triple[:, 0].astype(jnp.float32), 0) * query_scale,
            jnp.sum(grad_triple[:, 2].astype(jnp.float32), 0),
        ]
    )
    query_part = (
        jnp.einsum("tk,ck->tc", grad_triple[:, 0], qkv_w[:, 0], preferred_element_type=jnp.float32)
        * query_scale
    )
    other_part = jnp.einsum(
        "tjk,cjk->tc", grad_triple[:, 1:], qkv_w[:, 1:], preferred_element_type=jnp.float32
    )
    grad_canvas = from_windows(
        (query_part + other_part).reshape(count, WIN * WIN, C), height, across
    )
    grad_normed = scatter_grad(jnp.roll(grad_canvas, (amount, amount), (0, 1))[None])
    grad_gain_one = jnp.sum(grad_normed * scaled_one, (0, 1, 2))
    grad_offset_one = jnp.sum(grad_normed, (0, 1, 2))
    grad_input = grad_hidden + norm_back(grad_normed, scaled_one, factor_one, gain_pair[0])
    shared = (
        jnp.stack([grad_gain_one, grad_gain_two]),
        jnp.stack([grad_offset_one, grad_offset_two]),
        grad_proj_b,
        grad_fc2_b,
    )
    sharded = (grad_qkv_w, grad_qv_b, grad_proj_w, grad_fc1_w, grad_fc1_b, grad_fc2_w, grad_table)
    return (grad_input, shared, sharded)


def on_device(
    tokens,
    crop_ids,
    cotangent,
    norm_gain,
    norm_bias,
    qkv_weight,
    qv_bias,
    proj_weight,
    proj_bias,
    fc1_weight,
    fc1_bias,
    fc2_weight,
    fc2_bias,
    pos_table,
):
    onehot = table_map()
    crop_grid = crop_ids[0]
    every_weight = (
        norm_gain,
        norm_bias,
        qkv_weight,
        qv_bias,
        proj_weight,
        proj_bias,
        fc1_weight,
        fc1_bias,
        fc2_weight,
        fc2_bias,
        pos_table,
    )
    states = tokens.astype(jnp.float32)
    inputs = []
    stored_all = []
    for number in range(LAYERS):
        inputs.append(states)
        layer_weights = tuple((item[number] for item in every_weight))
        states, stored = layer_forward(states, crop_grid, layer_weights, number % 2 == 1, onehot)
        stored_all.append(stored)
    layer_out = states.astype(jnp.bfloat16)
    grad_rows = cotangent.astype(jnp.float32)
    shared_list = [None] * LAYERS
    sharded_list = [None] * LAYERS
    for number in reversed(range(LAYERS)):
        layer_weights = tuple((item[number] for item in every_weight))
        unused, stored = layer_forward(
            inputs[number], crop_grid, layer_weights, number % 2 == 1, onehot
        )
        grad_rows, shared, sharded = layer_backward(
            grad_rows, stored, layer_weights, number % 2 == 1, onehot
        )
        shared_list[number] = shared
        sharded_list[number] = sharded
    shared_all = tuple((jnp.stack([entry[place] for entry in shared_list]) for place in range(4)))
    sharded_all = tuple((jnp.stack([entry[place] for entry in sharded_list]) for place in range(7)))
    sharded_all = lax.psum(sharded_all, "win")
    shared_all = lax.psum(shared_all, ("win", "tp"))
    return (
        layer_out,
        grad_rows,
        shared_all[0],
        shared_all[1],
        sharded_all[0],
        sharded_all[1],
        sharded_all[2],
        shared_all[2],
        sharded_all[3],
        sharded_all[4],
        sharded_all[5],
        shared_all[3],
        sharded_all[6],
    )


def solution(mesh):
    return jax.shard_map(
        on_device,
        mesh=mesh,
        in_specs=(
            P("win", "tp", None, None),
            P("win", None, None),
            P("win", "tp", None, None),
            P(),
            P(),
            P(None, None, None, "tp"),
            P(None, None, "tp"),
            P(None, "tp", None),
            P(),
            P(None, None, "tp"),
            P(None, "tp"),
            P(None, "tp", None),
            P(),
            P(None, None, "tp"),
        ),
        out_specs=(
            P("win", "tp", None, None),
            P("win", "tp", None, None),
            P(),
            P(),
            P(None, None, None, "tp"),
            P(None, None, "tp"),
            P(None, "tp", None),
            P(),
            P(None, None, "tp"),
            P(None, "tp"),
            P(None, "tp", None),
            P(),
            P(None, None, "tp"),
        ),
        check_vma=False,
    )
```

profile of v0, /device:TPU:0, one launch (start us, length us, event | category | flops | bytes accessed | tf_op | source)
XLA Modules:
  0.0 1144.6 jit_solution(10286683492717790055)
XLA Ops:
  19.2 21.5 %all-gather.9.cloned.1.call-done = bf16[1,56,28,384]{3,2,0,1:T(8,128)(2,1)} async-done(((bf16[1,28,28,384]{3,2,0,1:T(8,128)(2,1)}), bf16[1,56,28,384]{3,2,0,1:T(8,128)(2,1)}) %all-gather.9.cloned.1.call-update) | async-done | bytes 1204240 | tf_op jit(solution)/shard_map/all_gather | solution.py:95
  66.7 6.8 copy.223
  84.8 67.4 %all-reduce.21.cloned.1.call-done = f32[1,56,28,384]{3,0,2,1:T(1,128)} async-done(((f32[1,56,28,384]{3,0,2,1:T(1,128)}), f32[1,56,28,384]{3,0,2,1:T(1,128)}) %all-reduce.21.cloned.1.call-update) | async-done | bytes 2408464
  156.9 24.5 %all-gather.11.cloned.1.call-done = bf16[1,56,28,384]{3,2,0,1:T(8,128)(2,1)} async-done(((bf16[1,28,28,384]{3,2,0,1:T(8,128)(2,1)}), bf16[1,56,28,384]{3,2,0,1:T(8,128)(2,1)}) %all-gather.11.cloned.1.call-update) | async-done | bytes 1204240 | tf_op jit(solution)/shard_map/all_gather | solution.py:142
  183.6 14.2 %multiply_convert_fusion.1 = (bf16[1568,768]{1,0:T(8,128)(2,1)}, f32[1568,768]{1,0:T(8,128)}, f32[1568,768]{1,0:T(8,128)}) fusion(f32[768]{0:T(1024)S(1)} %get-tuple-element.82, bf16[1568,384]{1,0:T(8,128)(2,1)S(1)} %reshape.632, bf16[2,384,768]{2,1,0:T(8,128)(2,1)} %param.25), kind=kOutput, calls=%fused_computation.31 | convolution fusion | flops 1004322816 | bytes 13839360 | tf_op jit(solution)/shard_map/dot_general | solution.py:144
  208.6 42.6 %all-reduce.23.cloned.1.call-done = bf16[1,56,28,384]{3,1,2,0:T(8,128)(2,1)} async-done(((bf16[1,56,28,384]{3,1,2,0:T(8,128)(2,1)}), bf16[1,56,28,384]{3,1,2,0:T(8,128)(2,1)}) %all-reduce.23.cloned.1.call-update) | async-done | bytes 1204240
  260.1 20.6 %all-gather.13.cloned.1.call-done = bf16[1,56,28,384]{3,2,0,1:T(8,128)(2,1)} async-done(((bf16[1,28,28,384]{3,2,0,1:T(8,128)(2,1)}), bf16[1,56,28,384]{3,2,0,1:T(8,128)(2,1)}) %all-gather.13.cloned.1.call-update) | async-done | bytes 1204240 | tf_op jit(solution)/shard_map/all_gather | solution.py:95
  307.9 6.8 copy.242
  329.3 69.0 %all-reduce.25.cloned.1.call-done = f32[1,56,28,384]{3,0,2,1:T(1,128)} async-done(((f32[1,56,28,384]{3,0,2,1:T(1,128)}), f32[1,56,28,384]{3,0,2,1:T(1,128)}) %all-reduce.25.cloned.1.call-update) | async-done | bytes 2408464
  402.4 22.5 %all-gather.17.cloned.1.call-done = bf16[1,56,28,384]{3,2,0,1:T(8,128)(2,1)} async-done(((bf16[1,28,28,384]{3,2,0,1:T(8,128)(2,1)}), bf16[1,56,28,384]{3,2,0,1:T(8,128)(2,1)}) %all-gather.17.cloned.1.call-update) | async-done | bytes 1204240 | tf_op jit(solution)/shard_map/all_gather | solution.py:78
  427.9 24.2 %all-gather.15.cloned.1.call-done = bf16[1,56,28,384]{3,2,0,1:T(8,128)(2,1)} async-done(((bf16[1,28,28,384]{3,2,0,1:T(8,128)(2,1)}), bf16[1,56,28,384]{3,2,0,1:T(8,128)(2,1)}) %all-gather.15.cloned.1.call-update) | async-done | bytes 1204240 | tf_op jit(solution)/shard_map/all_gather | solution.py:142
  455.1 36.5 %multiply_convert_fusion = (bf16[1568,768]{1,0:T(8,128)(2,1)}, f32[1568,768]{1,0:T(8,128)S(1)}, f32[1568,768]{1,0:T(8,128)S(1)}) fusion(f32[768]{0:T(1024)S(1)} %copy-done.105, bf16[1568,384]{1,0:T(8,128)(2,1)} %reshape.635, bf16[2,384,768]{2,1,0:T(8,128)(2,1)} %param.25), kind=kOutput, calls=%fused_computation.18 | convolution fusion | flops 1004322816 | bytes 13839360 | tf_op jit(solution)/shard_map/dot_general | solution.py:144
  491.6 5.2 convert_reduce_fusion
  506.6 43.4 %all-reduce.27.cloned.1.call-done = bf16[1,56,28,384]{3,1,2,0:T(8,128)(2,1)} async-done(((bf16[1,56,28,384]{3,1,2,0:T(8,128)(2,1)}), bf16[1,56,28,384]{3,1,2,0:T(8,128)(2,1)}) %all-reduce.27.cloned.1.call-update) | async-done | bytes 1204240
  558.4 23.1 %all-gather.19.cloned.1.call-done = bf16[1,56,28,384]{3,2,0,1:T(8,128)(2,1)} async-done(((bf16[1,28,28,384]{3,2,0,1:T(8,128)(2,1)}), bf16[1,56,28,384]{3,2,0,1:T(8,128)(2,1)}) %all-gather.19.cloned.1.call-update) | async-done | bytes 1204240 | tf_op jit(solution)/shard_map/all_gather | solution.py:78
  597.2 6.5 reshape.637
  603.7 6.5 convert_reduce_fusion.2
  610.2 5.7 multiply_reduce_fusion.1
  661.9 43.5 %all-reduce.29.cloned.1.call-done = bf16[1,56,28,384]{3,1,2,0:T(8,128)(2,1)} async-done(((bf16[1,56,28,384]{3,1,2,0:T(8,128)(2,1)}), bf16[1,56,28,384]{3,1,2,0:T(8,128)(2,1)}) %all-reduce.29.cloned.1.call-update) | async-done | bytes 1204240
  712.0 25.2 %all-gather.21.cloned.1.call-done = bf16[1,56,28,384]{3,2,0,1:T(8,128)(2,1)} async-done(((bf16[1,28,28,384]{3,2,0,1:T(8,128)(2,1)}), bf16[1,56,28,384]{3,2,0,1:T(8,128)(2,1)}) %all-gather.21.cloned.1.call-update) | async-done | bytes 1204240 | tf_op jit(solution)/shard_map/all_gather | solution.py:78
  739.6 7.4 convert_reduce_fusion.1
  751.8 5.0 fusion.83
  775.0 4.9 dot_general.178
  786.7 13.7 %all-reduce.31.cloned.1.call-done = bf16[1,56,28,384]{3,1,2,0:T(8,128)(2,1)} async-done(((bf16[1,56,28,384]{3,1,2,0:T(8,128)(2,1)}), bf16[1,56,28,384]{3,1,2,0:T(8,128)(2,1)}) %all-reduce.31.cloned.1.call-update) | async-done | bytes 1204240
  805.3 5.0 fusion.89
  823.6 6.9 all-gather.23.cloned.1.call-done
  842.1 6.5 reshape.640
  848.6 6.5 convert_reduce_fusion.4
  855.2 5.7 multiply_reduce_fusion
  948.8 62.2 %all-reduce.9 = (f32[2,2,192]{2,1,0:T(2,128)}, f32[2,768]{1,0:T(2,128)}, f32[2,169,6]{1,2,0:T(8,128)}) all-reduce(f32[2,2,192]{2,1,0:T(2,128)} %pad_maximum_fusion.16, f32[2,768]{1,0:T(2,128)} %pad_maximum_fusion.15, f32[2,169,6]{1,2,0:T(8,128)S(1)} %pad_maximum_fusion.12), channel_id=1, replica_groups=mesh['win'=16,'tp'=2] {'win'}, use_global_device_ids=true, to_apply=%region_45.46 | all-reduce | flops 4332 | bytes 34656 | tf_op jit(solution)/shard_map/psum | solution.py:337
  1019.9 37.8 %all-reduce.8 = (f32[2,2,384]{2,1,0:T(2,128)}, f32[2,2,384]{2,1,0:T(2,128)}, f32[2,384]{1,0:T(2,128)}, f32[2,384]{1,0:T(2,128)}) all-reduce(f32[2,2,384]{2,1,0:T(2,128)S(1)} %pad_maximum_fusion.13, f32[2,2,384]{2,1,0:T(2,128)S(1)} %pad_maximum_fusion.14, f32[2,384]{1,0:T(2,128)S(1)} %copy-done.85, ...), channel_id=1, replica_groups=mesh['win'=16,'tp'=2] {'win','tp'}, use_global_device_ids=true, to_apply=%region_34.35 | all-reduce | flops 4608 | bytes 36864 | tf_op jit(solution)/shard_map/psum | solution.py:338
  1059.2 71.0 %all-reduce.33.cloned.1.call-done = (f32[2,384,3,192]{1,3,2,0:T(8,128)}, f32[2,192,384]{2,1,0:T(8,128)}, f32[2,384,768]{2,1,0:T(8,128)}, f32[2,768,384]{2,1,0:T(8,128)}) async-done(((f32[2,384,3,192]{1,3,2,0:T(8,128)}, f32[2,192,384]{2,1,0:T(8,128)}, f32[2,384,768]{2,1,0:T(8,128)}, f32[2,768,384]{2,1,0:T(8,128)}), (f32[2,384,3,192]{1,3,2,0:T(8,128)}, f32[2,192,384]{2,1,0:T(8,128)}, ...) | async-done | bytes 7077904 | tf_op jit(solution)/shard_map/psum | solution.py:337
  (528 shorter events, 379.6 us)
Async XLA Ops:
  7.2 33.5 %all-gather.9.cloned.1.call-start = ((), (), s32[]{:S(2)}) async-start(), calls=%async_computation | async-start | bytes 2064384 | tf_op jit(solution)/shard_map/all_gather | solution.py:95
  11.6 143.4 %copy-start.77 = (f32[384]{0:T(512)}, f32[384]{0:T(512)S(1)}, u32[]{:S(2)}) copy-start(f32[384]{0:T(512)S(1)} %get-tuple-element.168) | copy-start | bytes 4612
  12.8 139.3 %all-reduce.21.cloned.1.call-start = ((), (), s32[]{:S(2)}) async-start(), calls=%async_computation.8 | async-start | bytes 4816896
  82.3 72.0 %copy-start.9 = (bf16[1,28,28,384]{3,2,1,0:T(8,128)(2,1)S(1)}, bf16[1,28,28,384]{3,2,1,0:T(8,128)(2,1)}, u32[]{:S(2)}) copy-start(bf16[1,28,28,384]{3,2,1,0:T(8,128)(2,1)} %param.16) | copy-start | bytes 1806340
  82.3 99.1 %all-gather.11.cloned.1.call-start = ((), (), s32[]{:S(2)}) async-start(), calls=%async_computation.1 | async-start | bytes 2064384 | tf_op jit(solution)/shard_map/all_gather | solution.py:142
  154.6 98.1 %copy-start = (f32[1,28,28,384]{3,2,0,1:T(8,128)}, f32[1,28,28,384]{3,2,0,1:T(8,128)S(1)}, u32[]{:S(2)}) copy-start(f32[1,28,28,384]{3,2,0,1:T(8,128)S(1)} %get-tuple-element.128) | copy-start | bytes 3612676
  156.2 95.0 %all-reduce.23.cloned.1.call-start = ((), (), s32[]{:S(2)}) async-start(), calls=%async_computation.9 | async-start | bytes 2408448
  156.9 40.9 %copy-start.103 = (f32[768]{0:T(1024)}, f32[768]{0:T(1024)S(1)}, u32[]{:S(2)}) copy-start(f32[768]{0:T(1024)S(1)} %get-tuple-element.82) | copy-start | bytes 9220
  207.6 73.1 %all-gather.13.cloned.1.call-start = ((), (), s32[]{:S(2)}) async-start(), calls=%async_computation.2 | async-start | bytes 2064384 | tf_op jit(solution)/shard_map/all_gather | solution.py:95
  208.0 95.2 %copy-start.108 = (f32[6,32]{1,0:T(8,128)}, f32[6,32]{1,0:T(8,128)S(1)}, u32[]{:S(2)}) copy-start(f32[6,32]{1,0:T(8,128)S(1)} %add.485) | copy-start | bytes 2308
  255.5 142.9 %all-reduce.25.cloned.1.call-start = ((), (), s32[]{:S(2)}) async-start(), calls=%async_computation.10 | async-start | bytes 4816896
  328.5 72.0 %copy-start.3 = (f32[1,28,28,384]{3,2,0,1:T(8,128)S(1)}, f32[1,28,28,384]{3,2,0,1:T(8,128)}, u32[]{:S(2)}) copy-start(f32[1,28,28,384]{3,2,0,1:T(8,128)} %copy-done.2) | copy-start | bytes 3612676
  328.5 72.0 %copy-start.89 = (f32[384]{0:T(512)S(1)}, f32[384]{0:T(512)}, u32[]{:S(2)}) copy-start(f32[384]{0:T(512)} %get-tuple-element.97) | copy-start | bytes 4612
  328.5 96.4 %all-gather.17.cloned.1.call-start = ((), (), s32[]{:S(2)}) async-start(), calls=%async_computation.4 | async-start | bytes 2064384 | tf_op jit(solution)/shard_map/all_gather | solution.py:78
  329.3 122.8 %all-gather.15.cloned.1.call-start = ((), (), s32[]{:S(2)}) async-start(), calls=%async_computation.3 | async-start | bytes 2064384 | tf_op jit(solution)/shard_map/all_gather | solution.py:142
  402.4 147.6 %all-reduce.27.cloned.1.call-start = ((), (), s32[]{:S(2)}) async-start(), calls=%async_computation.11 | async-start | bytes 2408448
  427.9 27.2 %copy-start.105 = (f32[768]{0:T(1024)S(1)}, f32[768]{0:T(1024)}, u32[]{:S(2)}) copy-start(f32[768]{0:T(1024)} %get-tuple-element.81) | copy-start | bytes 9220
  455.0 36.5 %copy-start.44 = (bf16[1568,384]{1,0:T(8,128)(2,1)S(1)}, bf16[1568,384]{1,0:T(8,128)(2,1)}, u32[]{:S(2)}) copy-start(bf16[1568,384]{1,0:T(8,128)(2,1)} %reshape_squeeze.16) | copy-start | bytes 3612676
  455.0 36.5 %copy-start.119 = (bf16[2,768,384]{2,1,0:T(8,128)(2,1)S(1)}, bf16[2,768,384]{2,1,0:T(8,128)(2,1)}, u32[]{:S(2)}) copy-start(bf16[2,768,384]{2,1,0:T(8,128)(2,1)} %param.27) | copy-start | bytes 3538948
  506.4 75.0 %all-gather.19.cloned.1.call-start = ((), (), s32[]{:S(2)}) async-start(), calls=%async_computation.5 | async-start | bytes 2064384 | tf_op jit(solution)/shard_map/all_gather | solution.py:78
  556.2 149.2 %all-reduce.29.cloned.1.call-start = ((), (), s32[]{:S(2)}) async-start(), calls=%async_computation.12 | async-start | bytes 2408448
  661.8 75.4 %all-gather.21.cloned.1.call-start = ((), (), s32[]{:S(2)}) async-start(), calls=%async_computation.6 | async-start | bytes 2064384 | tf_op jit(solution)/shard_map/all_gather | solution.py:78
  711.9 27.6 %copy-start.104 = (f32[768]{0:T(1024)S(1)}, f32[768]{0:T(1024)}, u32[]{:S(2)}) copy-start(f32[768]{0:T(1024)} %copy-done.103) | copy-start | bytes 9220
  712.0 88.4 %all-reduce.31.cloned.1.call-start = ((), (), s32[]{:S(2)}) async-start(), calls=%async_computation.13 | async-start | bytes 2408448
  756.8 73.6 %all-gather.23.cloned.1.call-start = ((), (), s32[]{:S(2)}) async-start(), calls=%async_computation.7 | async-start | bytes 2064384 | tf_op jit(solution)/shard_map/all_gather | solution.py:78
  805.2 207.1 %all-reduce.35.cloned.1.call-start = ((), (), s32[]{:S(2)}) async-start(), calls=%async_computation.15 | async-start | bytes 4816896
  902.7 227.5 %all-reduce.33.cloned.1.call-start = ((), (), s32[]{:S(2)}) async-start(), calls=%async_computation.14 | async-start | bytes 14155776 | tf_op jit(solution)/shard_map/psum | solution.py:337
  926.6 87.3 %copy-start.10 = (bf16[1,28,28,384]{3,2,1,0:T(8,128)(2,1)S(1)}, bf16[1,28,28,384]{3,2,1,0:T(8,128)(2,1)}, u32[]{:S(2)}) copy-start(bf16[1,28,28,384]{3,2,1,0:T(8,128)(2,1)} %param.16) | copy-start | bytes 1806340
  926.6 87.3 %copy-start.62 = (f32[28,28]{1,0:T(8,128)S(1)}, f32[28,28]{1,0:T(8,128)}, u32[]{:S(2)}) copy-start(f32[28,28]{1,0:T(8,128)} %copy-done.61) | copy-start | bytes 9412
  926.6 87.3 %copy-start.65 = (f32[28,28]{1,0:T(8,128)S(1)}, f32[28,28]{1,0:T(8,128)}, u32[]{:S(2)}) copy-start(f32[28,28]{1,0:T(8,128)} %copy-done.64) | copy-start | bytes 9412
  1017.5 40.2 %copy-start.63 = (bf16[1,56,28,384]{3,1,2,0:T(8,128)(2,1)S(1)}, bf16[1,56,28,384]{3,1,2,0:T(8,128)(2,1)}, u32[]{:S(2)}) copy-start(bf16[1,56,28,384]{3,1,2,0:T(8,128)(2,1)} %get-tuple-element.110) | copy-start | bytes 3612676
  1017.5 40.4 %copy-start.90 = (f32[384]{0:T(512)S(1)}, f32[384]{0:T(512)}, u32[]{:S(2)}) copy-start(f32[384]{0:T(512)} %get-tuple-element.95) | copy-start | bytes 4612
  (109 other events, 483.3 us)
Sparse Core Ops, SparseCore 0:
  13.0 27.6 all-gather.8
  82.4 69.6 all-reduce.20
  156.3 24.9 all-gather.10
  207.7 43.4 all-reduce.22
  255.6 25.0 all-gather.12
  328.6 69.6 all-reduce.24
  399.9 24.9 all-gather.16
  427.0 24.9 all-gather.14
  506.5 43.4 all-reduce.26
  556.3 25.0 all-gather.18
  662.0 43.4 all-reduce.28
  712.1 25.0 all-gather.20
  756.9 43.4 all-reduce.30
  805.3 25.0 all-gather.22
  902.8 69.8 all-reduce.34
  978.3 151.8 all-reduce.32
where the time goes:
time: 1150 us; the launch traced here: 1140 us
  waiting for transfers between devices  520 us (45%)
  local copies, waits for them, and re-layouts  270 us (23%)
  matrix products  178 us (15%)
  blocking collectives  100 us (9%)
  other arithmetic  59.4 us (5%)
  between operations  16.6 us (1%)
    unnamed x23, waiting for transfers between devices  281 us
    all_gather x4, waiting for transfers between devices, gather_grad(): lax.all_gather(grad_rows.astype(jnp.bfloat16), 'tp', axis=1, tiled=True)[0]  77.7 us
    psum x1, waiting for transfers between devices, on_device(): sharded_all = lax.psum(sharded_all, 'win')  71 us
    psum x1, blocking collectives, on_device(): sharded_all = lax.psum(sharded_all, 'win')  62.2 us
    dot_general x2, matrix products, layer_forward(): jnp.dot(flat_two, fc1_w, preferred_element_type=jnp.float32) + fc1_b  50.7 us
    all_gather x2, waiting for transfers between devices, layer_forward(): lax.all_gather(normed_two.astype(jnp.bfloat16), 'tp', axis=1, tiled=True)  48.6 us
    all_gather x2, waiting for transfers between devices, layer_forward(): gathered = lax.all_gather(normed_low, 'tp', axis=1, tiled=True)[0]  42.1 us
    psum x1, blocking collectives, on_device(): shared_all = lax.psum(shared_all, ('win', 'tp'))  37.8 us
  transfers between devices with their start and end apart: 16, of which 15 were waited for; matrix products, arithmetic and copies ran while one was open for 11% of the time, Pallas kernels for 0%

commit v1 on v0

v1 whole, which is shorter than its diff:
```python
from functools import partial

import jax
import jax.numpy as jnp
import numpy as np
from jax import lax
from jax.experimental import pallas as pl
from jax.experimental.pallas import tpu as pltpu
from jax.sharding import PartitionSpec as P

C = 384
WIN = 7
SHIFT = 3
HD = 32
EPS = 1e-05
NEG = -1000000000.0
SCALE = HD**-0.5
F32 = jnp.float32
BF = jnp.bfloat16
SEG = 8
WROWS = WIN * SEG
WPAD = 64
VMEM_LIMIT = 56 * 2**20


def nn(a, b):
    return lax.dot_general(a, b, (((1,), (0,)), ((), ())), preferred_element_type=F32)


def nt(a, b):
    return lax.dot_general(a, b, (((1,), (1,)), ((), ())), preferred_element_type=F32)


def tn(a, b):
    return lax.dot_general(a, b, (((0,), (0,)), ((), ())), preferred_element_type=F32)


def norm_stats(x):
    mean = jnp.mean(x, -1, keepdims=True)
    cent = x - mean
    var = jnp.mean(cent * cent, -1, keepdims=True)
    rinv = lax.rsqrt(var + EPS)
    return cent * rinv, rinv


def norm_back(dz, xhat, rinv, gain):
    d = dz * gain
    return rinv * (
        d - jnp.mean(d, -1, keepdims=True) - xhat * jnp.mean(d * xhat, -1, keepdims=True)
    )


def tile_row(r, k, across):
    return (((r // WIN) * across + k) * WIN + r % WIN) * SEG


def zero_rows(n):
    return jnp.zeros((n, C), F32)


def head_mask():
    row = lax.broadcasted_iota(jnp.int32, (6 * WPAD, 6 * HD), 0) // WPAD
    col = lax.broadcasted_iota(jnp.int32, (6 * WPAD, 6 * HD), 1) // HD
    return (row == col).astype(BF)


def spread(x, mask):
    return jnp.concatenate([x] * 6, axis=0) * mask


def swap_heads(x):
    parts = []
    for i in range(3):
        t = x[:, 128 * i : 128 * (i + 1)].T
        parts.append(jnp.concatenate([t[:WPAD], t[WPAD:]], axis=1))
    return jnp.concatenate(parts, axis=1)


def shift_in(tile, x_ref, rows, across):
    for r in range(rows):
        for k in range(across):
            a = tile(r + SHIFT, k)
            b = tile(r + SHIFT, (k + 1) % across)
            x_ref[pl.ds(tile_row(r, k, across), SEG), :] = jnp.concatenate(
                [a[SHIFT:WIN], b[:SHIFT], zero_rows(1)], axis=0
            )


def shift_out(tile, x_ref, rows, across):
    for r in range(rows):
        for k in range(across):
            a = tile(r - SHIFT, (k - 1) % across)
            b = tile(r - SHIFT, k)
            x_ref[pl.ds(tile_row(r, k, across), SEG), :] = jnp.concatenate(
                [a[WIN - SHIFT : WIN], b[: WIN - SHIFT], zero_rows(1)], axis=0
            )


def attn_fwd_kernel(layer, rows, across, *refs):
    if layer == 0:
        (tok_ref, refs) = (refs[0], refs[1:])
    else:
        (st_ref, halo_ref, refs) = (refs[0], refs[1], refs[2:])
    (gain_ref, bias_ref, pb_ref, own_ref, oa_ref, ob_ref, qvb_ref, pos_ref, lq_ref, lk_ref) = refs[
        :10
    ]
    (x_ref, hid_ref, xn_ref, qkv_ref, p_ref, mix_ref, mask_ref) = refs[10:]
    wins = (rows // WIN) * across
    if layer == 0:
        for r in range(rows):
            row = tok_ref[r].astype(F32)
            for k in range(across):
                x_ref[pl.ds(tile_row(r, k, across), SEG), :] = jnp.concatenate(
                    [row[WIN * k : WIN * (k + 1)], zero_rows(1)], axis=0
                )
    else:

        def tile(r, k):
            if r < rows:
                return st_ref[pl.ds(tile_row(r, k, across), SEG), :]
            return halo_ref[k, r - rows]

        shift_in(tile, x_ref, rows, across)
    mask_ref[...] = head_mask()
    gain = gain_ref[layer, 0:1]
    bias = bias_ref[layer, 0:1]

    def norm_one(w, carry):
        x = x_ref[pl.ds(pl.multiple_of(w * WROWS, WROWS), WROWS), :]
        xhat, _ = norm_stats(x)
        xn = jnp.concatenate([xhat * gain + bias, zero_rows(WPAD - WROWS)], axis=0)
        xn_ref[pl.ds(pl.multiple_of(w * WPAD, WPAD), WPAD), :] = xn.astype(BF)
        return carry

    lax.fori_loop(0, wins, norm_one, 0)

    def weight(half, j):
        if half == 0:
            return jnp.concatenate(
                [own_ref[0, 96 * j : 96 * (j + 1)], own_ref[1, 96 * j : 96 * (j + 1)]], axis=0
            )
        return jnp.concatenate(
            [oa_ref[96 * j : 96 * (j + 1)], ob_ref[96 * j : 96 * (j + 1)]], axis=0
        )

    big = 4 * WPAD

    def project(i, carry):
        at = pl.ds(pl.multiple_of(i * big, big), big)
        xn = xn_ref[at, :]
        for half in range(2):
            q = nt(xn, weight(half, 0))
            qkv_ref[half, 0, at, :] = ((q + qvb_ref[half, 0:1]) * SCALE).astype(BF)
            qkv_ref[half, 1, at, :] = nt(xn, weight(half, 1)).astype(BF)
            v = nt(xn, weight(half, 2))
            qkv_ref[half, 2, at, :] = (v + qvb_ref[half, 1:2]).astype(BF)
        return carry

    lax.fori_loop(0, wins // 4, project, 0)

    def attend(w, carry):
        at = pl.ds(pl.multiple_of(w * WPAD, WPAD), WPAD)
        same = lk_ref[w] == lq_ref[pl.ds(w, 1), :]
        same = jnp.concatenate([same] * 3, axis=1)
        for half in range(2):
            q = qkv_ref[half, 0, at, :]
            k = qkv_ref[half, 1, at, :]
            v = qkv_ref[half, 2, at, :]
            s = nt(k, spread(q, mask_ref[...]))
            s = jnp.where(same, s + pos_ref[half], NEG)
            e = jnp.exp(s - jnp.max(s, 0, keepdims=True))
            p = (e / jnp.sum(e, 0, keepdims=True)).astype(BF)
            p_ref[half, w] = p
            mix_ref[half, at, :] = nn(swap_heads(p), spread(v, mask_ref[...])).astype(BF)
        return carry

    lax.fori_loop(0, wins, attend, 0)
    pb = pb_ref[layer : layer + 1]
    po = jnp.concatenate([own_ref[0, 288:384], own_ref[1, 288:384]], axis=0)
    pt = jnp.concatenate([oa_ref[288:384], ob_ref[288:384]], axis=0)

    def out(i, carry):
        at = pl.ds(pl.multiple_of(i * big, big), big)
        res = nn(mix_ref[0, at, :], po) + nn(mix_ref[1, at, :], pt) + pb
        for n in range(4):
            to = pl.ds(pl.multiple_of((i * 4 + n) * WROWS, WROWS), WROWS)
            hid_ref[to, :] = x_ref[to, :] + res[n * WPAD : n * WPAD + WROWS]
        return carry

    lax.fori_loop(0, wins // 4, out, 0)


BLK = 128


def mlp_fwd_kernel(
    layer,
    hid_ref,
    gain_ref,
    bias_ref,
    fb1_ref,
    fb2_ref,
    f1_ref,
    f2_ref,
    oa_ref,
    ob_ref,
    st_ref,
    act_ref,
    gp_ref,
):
    gain = gain_ref[layer, 1:2]
    bias = bias_ref[layer, 1:2]
    fb2 = fb2_ref[layer : layer + 1]

    def block(i, carry):
        at = pl.ds(pl.multiple_of(i * BLK, BLK), BLK)
        h = hid_ref[at, :]
        xhat, _ = norm_stats(h)
        n2 = (xhat * gain + bias).astype(BF)
        acc = h + fb2
        for q in range(4):
            w1, w2 = quarter(q, f1_ref, f2_ref, oa_ref, ob_ref)
            u = nn(n2, w1) + fb1_ref[q : q + 1]
            phi = 0.5 + 0.5 * lax.erf(u * (2.0**-0.5))
            act = (u * phi).astype(BF)
            act_ref[q, at, :] = act
            gp_ref[q, at, :] = (phi + u * (jnp.exp(-0.5 * u * u) * (2.0 * np.pi) ** -0.5)).astype(BF)
            acc = acc + nn(act, w2)
        st_ref[at, :] = acc
        return carry

    lax.fori_loop(0, hid_ref.shape[0] // BLK, block, 0)


def quarter(q, f1_ref, f2_ref, oa_ref, ob_ref):
    if q < 2:
        return f1_ref[:, C * q : C * (q + 1)], f2_ref[C * q : C * (q + 1), :]
    ref = oa_ref if q == 2 else ob_ref
    return ref[:C], ref[C:]


def mlp_bwd_kernel(layer, rows, across, *refs):
    (g_in_ref, halo_ref, hid_ref, act_ref, gp_ref, gain_ref, bias_ref) = refs[:7]
    (f1_ref, f2_ref, oa_ref, ob_ref, par_ref) = refs[7:12]
    (gh_ref, keep_ref, send_ref, fb1_ref, sh_ref) = refs[12:17]
    (g_ref, df_ref, n2_ref, du_ref) = refs[17:]
    if layer == 1:
        for r in range(rows):
            s = r + SHIFT
            row = (g_in_ref[s] if s < rows else halo_ref[s - rows]).astype(F32)
            for k in range(across):
                a = WIN * k + SHIFT
                if k < across - 1:
                    piece = [row[a : a + WIN]]
                else:
                    piece = [row[a:], row[:SHIFT]]
                g_ref[pl.ds(tile_row(r, k, across), SEG), :] = jnp.concatenate(
                    piece + [zero_rows(1)], axis=0
                )
    else:

        def tile(r, k):
            if r >= 0:
                return g_in_ref[pl.ds(tile_row(r, k, across), SEG), :]
            return halo_ref[k, r + SHIFT]

        shift_out(tile, g_ref, rows, across)
    gain = gain_ref[layer, 1:2]
    bias = bias_ref[layer, 1:2]

    def block(i, carry):
        sb, sg, sf, s1 = carry
        at = pl.ds(pl.multiple_of(i * BLK, BLK), BLK)
        g = g_ref[at, :]
        df = g.astype(BF)
        df_ref[at, :] = df
        sf = sf + jnp.sum(df.astype(F32), 0, keepdims=True)
        dz = None
        new = []
        for q in range(4):
            w1, w2 = quarter(q, f1_ref, f2_ref, oa_ref, ob_ref)
            du = (nt(df, w2) * gp_ref[q, at, :].astype(F32)).astype(BF)
            du_ref[q, at, :] = du
            new.append(s1[q] + jnp.sum(du.astype(F32), 0, keepdims=True))
            part = nt(du, w1)
            dz = part if dz is None else dz + part
        xhat, rinv = norm_stats(hid_ref[at, :])
        n2_ref[at, :] = (xhat * gain + bias).astype(BF)
        sg = sg + jnp.sum(dz * xhat, 0, keepdims=True)
        sb = sb + jnp.sum(dz, 0, keepdims=True)
        gh_ref[at, :] = g + norm_back(dz, xhat, rinv, gain)
        return sb, sg, sf, tuple(new)

    z = jnp.zeros((1, C), F32)
    sb, sg, sf, s1 = lax.fori_loop(
        0, hid_ref.shape[0] // BLK, block, (z, z, z, (z,) * 4)
    )
    for q in range(4):
        fb1_ref[q : q + 1] = s1[q]
    sh_ref[0:1] = sg
    sh_ref[1:2] = sb
    sh_ref[2:3] = sf
    par = par_ref[0]
    n2 = n2_ref[...]
    df = df_ref[...]
    for slot, ref in ((0, keep_ref), (1, send_ref)):
        for part in range(2):
            q = (par ^ slot) if part == 0 else 2 + slot
            ref[part, 0:C, :] = tn(n2, du_ref[q]).astype(BF)
            ref[part, C:, :] = tn(act_ref[q], df).astype(BF)


def attn_bwd_kernel(layer, rows, across, *refs):
    (gh_ref, x_ref, xn_ref, qkv_ref, p_ref, mix_ref, gain_ref) = refs[:7]
    (own_ref, oa_ref, ob_ref, par_ref) = refs[7:11]
    (gin_ref, keep_ref, send_ref, pos_ref, qvb_ref, sh_ref) = refs[11:17]
    (da_ref, do_ref, dqkv_ref, mask_ref, row_ref, gx_ref) = refs[17:]
    wins = (rows // WIN) * across
    gain = gain_ref[layer, 0:1]
    mask_ref[...] = head_mask()
    z = jnp.zeros((1, C), F32)

    def windowed(w, s):
        g = gh_ref[pl.ds(pl.multiple_of(w * WROWS, WROWS), WROWS), :]
        da = jnp.concatenate([g, zero_rows(WPAD - WROWS)], axis=0).astype(BF)
        da_ref[pl.ds(pl.multiple_of(w * WPAD, WPAD), WPAD), :] = da
        return s + jnp.sum(da.astype(F32), 0, keepdims=True)

    sh_ref[2:3] = lax.fori_loop(0, wins, windowed, z)
    big = 4 * WPAD
    po = jnp.concatenate([own_ref[0, 288:384], own_ref[1, 288:384]], axis=0)
    pt = jnp.concatenate([oa_ref[288:384], ob_ref[288:384]], axis=0)

    def mixed_grad(i, carry):
        at = pl.ds(pl.multiple_of(i * big, big), big)
        da = da_ref[at, :]
        do_ref[0, at, :] = nt(da, po).astype(BF)
        do_ref[1, at, :] = nt(da, pt).astype(BF)
        return carry

    lax.fori_loop(0, wins // 4, mixed_grad, 0)
    par = par_ref[0]

    def give(value, at, half):
        if half == 0:
            row_ref[...] = value
            one = row_ref[pl.ds(pl.multiple_of(par * 96, 96), 96), :]
            two = row_ref[pl.ds(pl.multiple_of((1 - par) * 96, 96), 96), :]
        else:
            one, two = value[:96], value[96:]
        keep_ref[half, at : at + 96, :] = one.astype(BF)
        send_ref[half, at : at + 96, :] = two.astype(BF)

    for half in range(2):
        give(tn(mix_ref[half], da_ref[...]), 288, half)
    pos_ref[...] = jnp.zeros_like(pos_ref)

    def attend(w, carry):
        at = pl.ds(pl.multiple_of(w * WPAD, WPAD), WPAD)
        for half in range(2):
            q = qkv_ref[half, 0, at, :]
            k = qkv_ref[half, 1, at, :]
            v = qkv_ref[half, 2, at, :]
            do = spread(do_ref[half, at, :], mask_ref[...])
            p = p_ref[half, w]
            pf = p.astype(F32)
            dp = nt(v, do)
            ds = pf * (dp - jnp.sum(pf * dp, 0, keepdims=True))
            pos_ref[half] += ds
            dsb = ds.astype(BF)
            dqkv_ref[half, 2, at, :] = nn(p, do).astype(BF)
            dqkv_ref[half, 1, at, :] = nn(dsb, spread(q, mask_ref[...])).astype(BF)
            dqkv_ref[half, 0, at, :] = nn(swap_heads(dsb), spread(k, mask_ref[...])).astype(BF)
        return carry

    lax.fori_loop(0, wins, attend, 0)

    def weight(half, j):
        if half == 0:
            return jnp.concatenate(
                [own_ref[0, 96 * j : 96 * (j + 1)], own_ref[1, 96 * j : 96 * (j + 1)]], axis=0
            )
        return jnp.concatenate(
            [oa_ref[96 * j : 96 * (j + 1)], ob_ref[96 * j : 96 * (j + 1)]], axis=0
        )

    def back(i, carry):
        sg, sb, sq = carry
        at = pl.ds(pl.multiple_of(i * big, big), big)
        dn = nn(dqkv_ref[0, 0, at, :], weight(0, 0)) + nn(dqkv_ref[1, 0, at, :], weight(1, 0))
        dn = dn * SCALE
        for half in range(2):
            for j in (1, 2):
                dn = dn + nn(dqkv_ref[half, j, at, :], weight(half, j))
        new = []
        for half in range(2):
            for n, j in enumerate((0, 2)):
                new.append(
                    sq[half * 2 + n]
                    + jnp.sum(dqkv_ref[half, j, at, :].astype(F32), 0, keepdims=True)
                )
        for n in range(4):
            to = pl.ds(pl.multiple_of((i * 4 + n) * WROWS, WROWS), WROWS)
            d = dn[n * WPAD : n * WPAD + WROWS]
            xhat, rinv = norm_stats(x_ref[to, :])
            sg = sg + jnp.sum(d * xhat, 0, keepdims=True)
            sb = sb + jnp.sum(d, 0, keepdims=True)
            gx_ref[to, :] = gh_ref[to, :] + norm_back(d, xhat, rinv, gain)
        return sg, sb, tuple(new)

    zq = jnp.zeros((1, 6 * HD), F32)
    sg, sb, sq = lax.fori_loop(0, wins // 4, back, (z, z, (zq,) * 4))
    sh_ref[0:1] = sg
    sh_ref[1:2] = sb
    for half in range(2):
        qvb_ref[half, 0:1] = sq[half * 2] * SCALE
        qvb_ref[half, 1:2] = sq[half * 2 + 1]
    xn = xn_ref[...]
    for half in range(2):
        for j in range(3):
            grad = tn(dqkv_ref[half, j], xn)
            give(grad * SCALE if j == 0 else grad, 96 * j, half)
    if layer == 1:
        gin_ref[...] = gx_ref[...]
    else:
        for r in range(rows):
            parts = [
                gx_ref[pl.ds(tile_row(r, k, across), SEG), :][:WIN] for k in range(across)
            ]
            gin_ref[r] = jnp.concatenate(parts, axis=0)


def out_kernel(rows, across, st_ref, halo_ref, o_ref):
    for r in range(rows):
        parts = []
        for k in range(across):
            if r >= SHIFT:
                t = st_ref[pl.ds(tile_row(r - SHIFT, k, across), SEG), :]
            else:
                t = halo_ref[k, r]
            parts.append(t[:WIN])
        last = parts[-1]
        parts = [last[WIN - SHIFT :]] + parts[:-1] + [last[: WIN - SHIFT]]
        o_ref[r] = jnp.concatenate(parts, axis=0).astype(BF)


def whole(x):
    return pl.BlockSpec(x.shape, lambda i, n=len(x.shape): (0,) * n)


def layer_of(x, layer):
    return pl.BlockSpec(
        (None,) + x.shape[1:], lambda i, n=len(x.shape): (layer,) + (0,) * (n - 1)
    )


SMEM = pl.BlockSpec(memory_space=pltpu.SMEM)


def call(kernel, name, operands, outs, scratch=()):
    args = []
    specs = []
    for op in operands:
        if isinstance(op, tuple):
            args.append(op[0])
            specs.append(op[1])
        else:
            args.append(op)
            specs.append(whole(op))
    shapes = [jax.ShapeDtypeStruct(s, d) for s, d in outs]
    return pl.pallas_call(
        kernel,
        name=name,
        grid=(1,),
        in_specs=specs,
        out_specs=[whole(s) for s in shapes],
        out_shape=shapes,
        scratch_shapes=list(scratch),
        compiler_params=pltpu.CompilerParams(vmem_limit_bytes=VMEM_LIMIT),
    )(*args)


def labels(crop_grid, shifted, tp_index, rows):
    height, across = crop_grid.shape
    grid = crop_grid
    if shifted:
        grid = jnp.roll(crop_grid, (-SHIFT, -SHIFT), (0, 1))
        row_ids = jnp.arange(height, dtype=jnp.int32)
        col_ids = jnp.arange(across, dtype=jnp.int32)
        zr = (row_ids >= height - WIN).astype(jnp.int32) + (row_ids >= height - SHIFT)
        zc = (col_ids >= across - WIN).astype(jnp.int32) + (col_ids >= across - SHIFT)
        grid = grid * 9 + zr[:, None] * 3 + zc[None, :]
    grid = lax.dynamic_slice(grid, (tp_index * rows, 0), (rows, across))
    lab = grid.reshape(rows // WIN, WIN, across // WIN, WIN).transpose(0, 2, 1, 3)
    lab = lab.reshape(-1, WIN, WIN)
    lab = jnp.pad(lab, ((0, 0), (0, 1), (0, 1)), constant_values=-1).reshape(-1, WPAD)
    return jnp.concatenate([lab, lab], 1), jnp.broadcast_to(lab[:, :, None], lab.shape + (128,))


def table_onehot():
    p = np.arange(WPAD)
    y, x = p // 8, p % 8
    dy = y[None, :] - y[:, None]
    dx = x[None, :] - x[:, None]
    real = (y < WIN) & (x < WIN)
    idx = (dy + WIN - 1) * (2 * WIN - 1) + dx + WIN - 1
    ok = real[None, :] & real[:, None]
    idx = np.where(ok, idx, -1).reshape(-1)
    return jnp.asarray(idx, jnp.int32)


def on_device(n_win, *args):
    (
        tokens,
        crop_ids,
        cotangent,
        norm_gain,
        norm_bias,
        qkv_weight,
        qv_bias,
        proj_weight,
        proj_bias,
        fc1_weight,
        fc1_bias,
        fc2_weight,
        fc2_bias,
        pos_table,
    ) = args
    rows, cols = tokens.shape[1:3]
    across = cols // WIN
    wins = (rows // WIN) * across
    ntok = wins * WROWS
    npad = wins * WPAD
    win = lax.axis_index("win")
    tp = lax.axis_index("tp")
    par = win % 2
    par_arr = par.astype(jnp.int32).reshape(1)
    bits = n_win.bit_length() - 1

    def to_tp(x):
        return lax.ppermute(x, "tp", [(0, 1), (1, 0)])

    def to_win(x, bit):
        return lax.ppermute(x, "win", [(i, i ^ (1 << bit)) for i in range(n_win)])

    qkv_t = qkv_weight.transpose(0, 2, 3, 1).reshape(2, 3, 2, 96, C).transpose(0, 2, 1, 3, 4)
    own_attn = jnp.concatenate(
        [qkv_t.reshape(2, 2, 288, C), proj_weight.reshape(2, 2, 96, C)], axis=2
    )
    attn_q = lax.dynamic_index_in_dim(own_attn, par, 1, keepdims=False)
    fc1_q = lax.dynamic_slice(fc1_weight, (0, 0, par * C), (2, C, C))
    fc2_q = lax.dynamic_slice(fc2_weight, (0, par * C, 0), (2, C, C))
    mlp_q = jnp.concatenate([fc1_q, fc2_q], axis=1)
    attn_a, attn_b, mlp_a, mlp_b = [], [], [], []
    for layer in range(2):
        a = to_tp(attn_q[layer])
        m = to_tp(mlp_q[layer])
        attn_a.append(a)
        mlp_a.append(m)
        attn_b.append(to_win(a, 0))
        mlp_b.append(to_win(m, 0))

    small = jnp.concatenate(
        [
            qv_bias.reshape(2, 2, 2, 96).transpose(2, 0, 1, 3).reshape(2, -1),
            fc1_bias.reshape(2, 2, C).transpose(1, 0, 2).reshape(2, -1),
            pos_table.transpose(2, 0, 1).reshape(2, -1),
        ],
        axis=1,
    )
    other = to_tp(small)
    other = jnp.where(par == 0, other, other[::-1])
    both = jnp.stack([small, other])
    n1, n2 = 2 * 2 * 96, 2 * C
    qvb = both[:, :, :n1].reshape(2, 2, 2, 2, 96).transpose(2, 0, 3, 1, 4).reshape(2, 2, 2, 192)
    fb1 = both[:, :, n1 : n1 + n2].reshape(2, 2, 2, C).transpose(2, 0, 1, 3).reshape(2, 4, C)
    table = both[:, :, n1 + n2 :].reshape(2, 2, 3, 2, -1)
    table = table.transpose(3, 0, 1, 2, 4).reshape(24, -1)
    onehot = (
        jnp.arange(table.shape[1], dtype=jnp.int32)[:, None] == table_onehot()[None, :]
    ).astype(F32)
    pos = jnp.dot(table, onehot, precision=lax.Precision.HIGHEST)
    pos = pos.reshape(2, 2, 6, WPAD, WPAD).transpose(0, 1, 3, 2, 4).reshape(2, 2, WPAD, 6 * WPAD)

    labs = [labels(crop_ids[0], layer == 1, tp, rows) for layer in range(2)]
    cot_halo = to_tp(cotangent[0, :SHIFT])

    tiles = (rows // WIN, across, WIN, SEG, C)

    saved = []
    src = (tokens[0],)
    for layer in range(2):
        lq, lk = labs[layer]
        own = (own_attn, layer_of(own_attn, layer))
        x, hid, xn, qkv, p, mix = call(
            partial(attn_fwd_kernel, layer, rows, across),
            "attn_fwd_%d" % layer,
            src
            + (norm_gain, norm_bias, proj_bias, own, attn_a[layer], attn_b[layer])
            + (qvb[layer], pos[layer], lq, lk),
            [
                ((ntok, C), F32),
                ((ntok, C), F32),
                ((npad, C), BF),
                ((2, 3, npad, 192), BF),
                ((2, wins, WPAD, 384), BF),
                ((2, npad, 192), BF),
            ],
            [pltpu.VMEM((6 * WPAD, 6 * HD), BF)],
        )
        f1 = (fc1_weight, layer_of(fc1_weight, layer))
        f2 = (fc2_weight, layer_of(fc2_weight, layer))
        st, act, gp = call(
            partial(mlp_fwd_kernel, layer),
            "mlp_fwd_%d" % layer,
            (hid, norm_gain, norm_bias, fb1[layer], fc2_bias, f1, f2, mlp_a[layer], mlp_b[layer]),
            [((ntok, C), F32), ((4, ntok, C), BF), ((4, ntok, C), BF)],
        )
        saved.append((x, hid, xn, qkv, p, mix, act, gp, own, f1, f2))
        if layer == 0:
            src = (st, to_tp(st.reshape(tiles)[0, :, :SHIFT]))
    halo = to_tp(st.reshape(tiles)[-1, :, WIN - SHIFT :])
    (layer_out,) = call(
        partial(out_kernel, rows, across), "layer_out", (st, halo), [((rows, cols, C), BF)]
    )

    def reduce_chunk(keep, send):
        got = to_win(send, 0)
        s = (keep.astype(F32) + got.astype(F32)).astype(BF)
        t = to_tp(s[1])
        acc = (s[0].astype(F32) + t.astype(F32)).astype(BF)
        for bit in range(1, bits):
            n = acc.shape[0] // 2
            b = (win >> bit) & 1
            mine = lax.dynamic_slice_in_dim(acc, b * n, n)
            away = lax.dynamic_slice_in_dim(acc, (1 - b) * n, n)
            acc = (mine.astype(F32) + to_win(away, bit).astype(F32)).astype(BF)
        for bit in reversed(range(1, bits)):
            b = (win >> bit) & 1
            got = to_win(acc, bit)
            acc = jnp.where(b == 0, jnp.concatenate([acc, got]), jnp.concatenate([got, acc]))
        return acc, to_win(acc, 0)

    g = (cotangent[0], cot_halo)
    chunks = [None, None]
    smalls = [None, None]
    for layer in (1, 0):
        x, hid, xn, qkv, p, mix, act, gp, own, f1, f2 = saved[layer]
        gh, keep_m, send_m, gfb1, sh2 = call(
            partial(mlp_bwd_kernel, layer, rows, across),
            "mlp_bwd_%d" % layer,
            g
            + (hid, act, gp, norm_gain, norm_bias, f1, f2, mlp_a[layer], mlp_b[layer])
            + ((par_arr, SMEM),),
            [
                ((ntok, C), F32),
                ((2, 2 * C, C), BF),
                ((2, 2 * C, C), BF),
                ((4, C), F32),
                ((3, C), F32),
            ],
            [
                pltpu.VMEM((ntok, C), F32),
                pltpu.VMEM((ntok, C), BF),
                pltpu.VMEM((ntok, C), BF),
                pltpu.VMEM((4, ntok, C), BF),
            ],
        )
        gin_shape = (ntok, C) if layer == 1 else (rows, cols, C)
        gin, keep_a, send_a, gpos, gqvb, sh1 = call(
            partial(attn_bwd_kernel, layer, rows, across),
            "attn_bwd_%d" % layer,
            (gh, x, xn, qkv, p, mix, norm_gain, own, attn_a[layer], attn_b[layer])
            + ((par_arr, SMEM),),
            [
                (gin_shape, F32),
                ((2, C, C), BF),
                ((2, C, C), BF),
                ((2, WPAD, 384), F32),
                ((2, 2, 192), F32),
                ((3, C), F32),
            ],
            [
                pltpu.VMEM((npad, C), BF),
                pltpu.VMEM((2, npad, 192), BF),
                pltpu.VMEM((2, 3, npad, 192), BF),
                pltpu.VMEM((6 * WPAD, 6 * HD), BF),
                pltpu.VMEM((192, C), F32),
                pltpu.VMEM((ntok, C), F32),
            ],
        )
        if layer == 1:
            g = (gin, to_tp(gin.reshape(tiles)[-1, :, WIN - SHIFT :]))
        chunks[layer] = (reduce_chunk(keep_m, send_m), reduce_chunk(keep_a, send_a))
        smalls[layer] = (gfb1, sh2, gpos, gqvb, sh1)

    gpos = jnp.stack([s[2] for s in smalls])
    gpos = gpos.reshape(2, 2, WPAD, 6, WPAD).transpose(0, 1, 3, 2, 4).reshape(24, -1)
    gtab = lax.dot_general(
        gpos, onehot, (((1,), (1,)), ((), ())), precision=lax.Precision.HIGHEST
    ).reshape(2, 2, 2, 3, -1)
    gqvb = jnp.stack([s[3] for s in smalls]).reshape(2, 2, 2, 2, 96).transpose(0, 1, 3, 2, 4)
    gfb1 = jnp.stack([s[0] for s in smalls]).reshape(2, 2, 2, C)
    pack = jnp.concatenate(
        [
            gqvb.transpose(1, 2, 0, 3, 4).reshape(2, 2, -1),
            gfb1.transpose(1, 2, 0, 3).reshape(2, 2, -1),
            gtab.transpose(1, 2, 0, 3, 4).reshape(2, 2, -1),
        ],
        axis=2,
    )
    theirs = jnp.where(par == 0, pack[1], pack[1][::-1])
    shared = jnp.stack([jnp.concatenate([s[4], s[1]]) for s in smalls])
    shared = shared + to_tp(shared)
    mine = pack[0] + to_tp(theirs)
    flat = jnp.concatenate([shared.reshape(-1), mine.reshape(-1)])
    size = flat.shape[0]
    flat = jnp.pad(flat, (0, -size % 1024)).reshape(-1, 128)
    for bit in range(bits):
        flat = flat + to_win(flat, bit)
    flat = flat.reshape(-1)[:size]
    shared = flat[: 12 * C].reshape(2, 6, C)
    mine = flat[12 * C :].reshape(2, -1)
    m1, m2 = 2 * 2 * 96, 2 * C
    out_qvb = mine[:, :m1].reshape(2, 2, 2, 96).transpose(1, 2, 0, 3).reshape(2, 2, 192)
    out_fb1 = mine[:, m1 : m1 + m2].reshape(2, 2, C).transpose(1, 0, 2).reshape(2, 2 * C)
    out_tab = mine[:, m1 + m2 :].reshape(2, 2, 3, -1).transpose(1, 3, 0, 2)
    out_tab = out_tab.reshape(2, -1, 6)

    def halves(pair):
        a, b = pair
        return jnp.where(par == 0, a, b).astype(F32), jnp.where(par == 0, b, a).astype(F32)

    gq, gp_, g1, g2 = [], [], [], []
    for layer in range(2):
        m0, m1 = halves(chunks[layer][0])
        a0, a1 = halves(chunks[layer][1])
        g1.append(jnp.concatenate([m0[:C], m1[:C]], axis=1))
        g2.append(jnp.concatenate([m0[C:], m1[C:]], axis=0))
        gp_.append(jnp.concatenate([a0[288:], a1[288:]], axis=0))
        q = jnp.stack([a0[:288].reshape(3, 96, C), a1[:288].reshape(3, 96, C)], axis=1)
        gq.append(q.reshape(3, 192, C).transpose(2, 0, 1))
    return (
        layer_out[None],
        gin[None],
        jnp.stack([shared[:, 0], shared[:, 3]], axis=1),
        jnp.stack([shared[:, 1], shared[:, 4]], axis=1),
        jnp.stack(gq),
        out_qvb,
        jnp.stack(gp_),
        shared[:, 2],
        jnp.stack(g1),
        out_fb1,
        jnp.stack(g2),
        shared[:, 5],
        out_tab,
    )


def solution(mesh):
    return jax.shard_map(
        partial(on_device, mesh.shape["win"]),
        mesh=mesh,
        in_specs=(
            P("win", "tp", None, None),
            P("win", None, None),
            P("win", "tp", None, None),
            P(),
            P(),
            P(None, None, None, "tp"),
            P(None, None, "tp"),
            P(None, "tp", None),
            P(),
            P(None, None, "tp"),
            P(None, "tp"),
            P(None, "tp", None),
            P(),
            P(None, None, "tp"),
        ),
        out_specs=(
            P("win", "tp", None, None),
            P("win", "tp", None, None),
            P(),
            P(),
            P(None, None, None, "tp"),
            P(None, None, "tp"),
            P(None, "tp", None),
            P(),
            P(None, None, "tp"),
            P(None, "tp"),
            P(None, "tp", None),
            P(),
            P(None, None, "tp"),
        ),
        check_vma=False,
    )
```

time: 1150 us -> 404 us (0.35)
  waiting for transfers between devices: 520 us -> 83.1 us
  local copies, waits for them, and re-layouts: 270 us -> 46.7 us
  Pallas kernels: 0 us -> 181 us
  matrix products: 178 us -> 4.14 us
  blocking collectives: 100 us -> 0 us
  starting transfers between devices: 0.84 us -> 60.1 us
  other arithmetic: 59.4 us -> 22.6 us
  between operations: 16.6 us -> 1.95 us
    unnamed x23 -> x0, waiting for transfers between devices: 281 us -> none
    pallas_call x0 -> x9, Pallas kernels: none -> 181 us  [call(): pl.pallas_call(kernel, name=name, grid=(1,), in_specs=specs, out_specs=[w...]
    dot_general x40 -> x2, matrix products: 174 us -> 4.14 us  [the longest x1 2.56 us: on_device(): pos = jnp.dot(table, onehot, precision=lax.Precision.HIGHEST)]
    all_gather x8 -> x0, waiting for transfers between devices: 168 us -> none  [the longest x4 77.7 us: gather_grad(): lax.all_gather(grad_rows.astype(jnp.bfloat16), 'tp', axis=1, tiled=True)[0]]
    psum x2 -> x0, blocking collectives: 100 us -> none  [the longest x1 62.2 us: on_device(): sharded_all = lax.psum(sharded_all, 'win')]
    ppermute x0 -> x55, waiting for transfers between devices: none -> 83.1 us  [the longest x40 52.4 us: to_win(): return lax.ppermute(x, 'win', [(i, i ^ 1 << bit) for i in range(n_win)])]
    psum x1 -> x0, waiting for transfers between devices: 71 us -> none  [on_device(): sharded_all = lax.psum(sharded_all, 'win')]
    convert_element_type x17 -> x0, local copies, waits for them, and re-layouts: 61.3 us -> none  [the longest x8 33.8 us: layer_forward(): mixed_low = mixed_heads.reshape(-1, local_cols).astype(jnp.bfloat16)]
  transfers between devices with their start and end apart: 16 -> 55, of which waited for: 15 -> 29; matrix products, arithmetic and copies ran while one was open for 11% -> 15% of each run, Pallas kernels for 0% -> 21%
where the time goes in v1:
time: 404 us; the launch traced here: 400 us
  Pallas kernels  181 us (45%)
  waiting for transfers between devices  83.1 us (21%)
  starting transfers between devices  60.1 us (15%)
  local copies, waits for them, and re-layouts  46.7 us (12%)
  other arithmetic  22.6 us (6%)
  matrix products  4.14 us (1%)
    pallas_call x9, Pallas kernels, call(): pl.pallas_call(kernel, name=name, grid=(1,), in_specs=specs, out_specs=[w...  181 us
    ppermute x40, waiting for transfers between devices, to_win(): return lax.ppermute(x, 'win', [(i, i ^ 1 << bit) for i in range(n_win)])  52.4 us
    ppermute x40, starting transfers between devices, to_win(): return lax.ppermute(x, 'win', [(i, i ^ 1 << bit) for i in range(n_win)])  44.2 us
    ppermute x15, waiting for transfers between devices, to_tp(): return lax.ppermute(x, 'tp', [(0, 1), (1, 0)])  30.6 us
    ppermute x15, starting transfers between devices, to_tp(): return lax.ppermute(x, 'tp', [(0, 1), (1, 0)])  15.9 us
    unnamed x72, local copies, waits for them, and re-layouts  10.9 us
  transfers between devices with their start and end apart: 55, of which 29 were waited for; matrix products, arithmetic and copies ran while one was open for 15% of the time, Pallas kernels for 21%

profile of v1, /device:TPU:0, one launch (start us, length us, event | category | flops | bytes accessed | tf_op | source)
XLA Modules:
  0.0 400.0 jit_solution(6933924718903748049)
XLA Ops:
  3.0 2.9 collective-permute-start
  20.4 5.9 %rev.6 = f32[2,2166]{1,0:T(2,128)S(1)} reverse(f32[2,2166]{1,0:T(2,128)} %collective-permute-done.2), dimensions={0} | reverse | bytes 34656 | tf_op jit(solution)/shard_map/rev | solution.py:572
  27.1 2.6 convolution_bitcast_fusion
  30.6 15.4 %collective-permute-done.8.oa_ref.refs_9_ = bf16[768,384]{1,0:T(8,128)(2,1)} collective-permute-done((bf16[768,384]{1,0:T(8,128)(2,1)}, bf16[768,384]{1,0:T(8,128)(2,1)}, u32[]{:S(2)}, u32[]{:S(2)}) %collective-permute-start.8) | collective-permute-done | bytes 589856 | tf_op jit(solution)/shard_map/ppermute | solution.py:541
  49.7 26.2 %attn_fwd_0.1 = (f32[896,384]{1,0:T(8,128)}, f32[896,384]{1,0:T(8,128)}, bf16[1024,384]{1,0:T(8,128)(2,1)}, bf16[2,3,1024,192]{3,2,1,0:T(8,128)(2,1)}, bf16[2,16...) custom-call(bf16[28,28,384]{2,1,0:T(8,128)(2,1)} %bitcast.195, f32[2,2,384]{2,1,0:T(2,128)} %refs_6_.7, ...), custom_call_target="tpu_custom_call" | custom-call | tf_op jit(solution)/shard_map/attn_fwd_0/pallas_call | solution.py:471
  76.7 14.9 %mlp_fwd_0.1 = (f32[896,384]{1,0:T(8,128)}, bf16[4,896,384]{2,1,0:T(8,128)(2,1)}, bf16[4,896,384]{2,1,0:T(8,128)(2,1)}) custom-call(f32[896,384]{1,0:T(8,128)} %get-tuple-element.53.hid_ref.refs_2_, f32[2,2,384]{2,1,0:T(2,128)} %refs_6_.7, f32[2,2,384]{2,1,0:T(2,128)} %refs_6_.6, f32[4,384]{1,0:T(4,128)} %squeeze.85.fb1_ref, f32[2,384]{1,0:T(2,128)} %fb2_ref.3, ...), custom_call_target="tpu_custom_call" | custom-call | tf_op jit(solution)/shard_map/mlp_fwd_0/pallas_call | solution.py:471
  99.4 26.7 %attn_fwd_1.1 = (f32[896,384]{1,0:T(8,128)}, f32[896,384]{1,0:T(8,128)}, bf16[1024,384]{1,0:T(8,128)(2,1)}, bf16[2,3,1024,192]{3,2,1,0:T(8,128)(2,1)}, bf16[2,16...) custom-call(f32[896,384]{1,0:T(8,128)} %get-tuple-element.54.refs_0_, f32[4,3,8,384]{3,2,1,0:T(8,128)} %copy-done.19, ...), custom_call_target="tpu_custom_call" | custom-call | tf_op jit(solution)/shard_map/attn_fwd_1/pallas_call | solution.py:471
  126.9 15.0 %mlp_fwd_1.1 = (f32[896,384]{1,0:T(8,128)}, bf16[4,896,384]{2,1,0:T(8,128)(2,1)}, bf16[4,896,384]{2,1,0:T(8,128)(2,1)}) custom-call(f32[896,384]{1,0:T(8,128)} %get-tuple-element.55.hid_ref.refs_2_, f32[2,2,384]{2,1,0:T(2,128)} %refs_6_.7, f32[2,2,384]{2,1,0:T(2,128)} %refs_6_.6, f32[4,384]{1,0:T(4,128)} %squeeze.91.fb1_ref, f32[2,384]{1,0:T(2,128)} %fb2_ref.3, ...), custom_call_target="tpu_custom_call" | custom-call | tf_op jit(solution)/shard_map/mlp_fwd_1/pallas_call | solution.py:471
  141.8 17.5 %mlp_bwd_1.1 = (f32[896,384]{1,0:T(8,128)}, bf16[2,768,384]{2,1,0:T(8,128)(2,1)}, bf16[2,768,384]{2,1,0:T(8,128)(2,1)}, f32[4,384]{1,0:T(4,128)}, f32[3,384]{1,0:T(4,128)}) custom-call(bf16[28,28,384]{2,1,0:T(8,128)(2,1)} %bitcast.194, bf16[3,28,384]{2,1,0:T(8,128)(2,1)} %collective-permute-done.11.refs_1_, f32[896,384]{1,0:T(8,128)} %get-tuple-element.55.hid_ref.refs_2_, ...), custom_call_target="tpu_custom_call" | custom-call | tf_op jit(solution)/shard_map/mlp_bwd_1/pallas_call | solution.py:471
  159.3 25.3 %attn_bwd_1.1 = (f32[896,384]{1,0:T(8,128)}, bf16[2,384,384]{2,1,0:T(8,128)(2,1)}, bf16[2,384,384]{2,1,0:T(8,128)(2,1)}, f32[2,64,384]{2,1,0:T(8,128)}, f32[2,2,192]{2,1,0:T(2,128)}, /*index=5*/f32[3,384]{1,0:T(4,128)}) custom-call(f32[896,384]{1,0:T(8,128)} %get-tuple-element.59.refs_0_, f32[896,384]{1,0:T(8,128)} %get-tuple-element.60.refs_1_, ...), custom_call_target="tpu_custom_call" | custom-call | tf_op jit(solution)/shard_map/attn_bwd_1/pallas_call | solution.py:471
  191.5 17.5 %mlp_bwd_0.1 = (f32[896,384]{1,0:T(8,128)}, bf16[2,768,384]{2,1,0:T(8,128)(2,1)}, bf16[2,768,384]{2,1,0:T(8,128)(2,1)}, f32[4,384]{1,0:T(4,128)}, f32[3,384]{1,0:T(4,128)}) custom-call(f32[896,384]{1,0:T(8,128)} %get-tuple-element.65.refs_0_, f32[4,3,8,384]{3,2,1,0:T(8,128)} %copy-done.20, f32[896,384]{1,0:T(8,128)} %get-tuple-element.53.hid_ref.refs_2_, ...), custom_call_target="tpu_custom_call" | custom-call | tf_op jit(solution)/shard_map/mlp_bwd_0/pallas_call | solution.py:471
  209.0 36.0 %attn_bwd_0.1 = (f32[28,28,384]{2,1,0:T(8,128)}, bf16[2,384,384]{2,1,0:T(8,128)(2,1)}, bf16[2,384,384]{2,1,0:T(8,128)(2,1)}, f32[2,64,384]{2,1,0:T(8,128)}, f32[2,2,192]{2,1,0:T(2,128)}, /*index=5*/f32[3,384]{1,0:T(4,128)}) custom-call(f32[896,384]{1,0:T(8,128)} %get-tuple-element.68.refs_0_, f32[896,384]{1,0:T(8,128)} %get-tuple-element.69.refs_1_, ...), custom_call_target="tpu_custom_call" | custom-call | tf_op jit(solution)/shard_map/attn_bwd_0/pallas_call | solution.py:471
  262.8 2.4 collective-permute-done.17
  265.8 2.6 collective-permute-start.18
  271.8 2.4 layer_out.1
  279.4 7.0 %collective-permute-done.29 = bf16[384,384]{1,0:T(8,128)(2,1)S(1)} collective-permute-done((bf16[384,384]{1,0:T(8,128)(2,1)S(1)}, bf16[384,384]{1,0:T(8,128)(2,1)S(1)}, u32[]{:S(2)}, u32[]{:S(2)}) %collective-permute-start.29) | collective-permute-done | bytes 294944 | tf_op jit(solution)/shard_map/ppermute | solution.py:541
  288.7 3.2 collective-permute-done.30
  293.7 2.8 collective-permute-done.20
  299.1 2.4 collective-permute-done.32
  317.5 4.2 %collective-permute-done.22 = bf16[96,384]{1,0:T(8,128)(2,1)S(1)} collective-permute-done((bf16[96,384]{1,0:T(8,128)(2,1)S(1)}, bf16[96,384]{1,0:T(8,128)(2,1)S(1)}, u32[]{:S(2)}, u32[]{:S(2)}) %collective-permute-start.22) | collective-permute-done | bytes 73760 | tf_op jit(solution)/shard_map/ppermute | solution.py:544
  324.5 2.3 collective-permute-done.23
  328.8 2.3 collective-permute-start.35
  332.1 4.0 %collective-permute-done.25 = bf16[96,384]{1,0:T(8,128)(2,1)S(1)} collective-permute-done((bf16[96,384]{1,0:T(8,128)(2,1)S(1)}, bf16[96,384]{1,0:T(8,128)(2,1)S(1)}, u32[]{:S(2)}, u32[]{:S(2)}) %collective-permute-start.25) | collective-permute-done | bytes 73760 | tf_op jit(solution)/shard_map/ppermute | solution.py:544
  338.3 3.1 collective-permute-done.26
  343.4 7.8 %collective-permute-done.48 = bf16[384,384]{1,0:T(8,128)(2,1)S(1)} collective-permute-done((bf16[384,384]{1,0:T(8,128)(2,1)S(1)}, bf16[384,384]{1,0:T(8,128)(2,1)S(1)}, u32[]{:S(2)}, u32[]{:S(2)}) %collective-permute-start.48) | collective-permute-done | bytes 294944 | tf_op jit(solution)/shard_map/ppermute | solution.py:544
  353.1 3.8 collective-permute-done.49
  357.0 2.7 collective-permute-start.50
  362.9 2.7 collective-permute-start.51
  372.2 2.5 collective-permute-start.42
  376.4 2.7 collective-permute-start.53
  381.0 2.8 collective-permute-done.53
  388.5 5.4 %collective-permute-done.44 = bf16[384,384]{1,0:T(8,128)(2,1)S(1)} collective-permute-done((bf16[384,384]{1,0:T(8,128)(2,1)S(1)}, bf16[384,384]{1,0:T(8,128)(2,1)S(1)}, u32[]{:S(2)}, u32[]{:S(2)}) %collective-permute-start.44) | collective-permute-done | bytes 294944 | tf_op jit(solution)/shard_map/ppermute | solution.py:544
  (346 shorter events, 123.1 us)
Async XLA Ops:
  3.0 27.0 %collective-permute-start = (bf16[384,384]{1,0:T(8,128)(2,1)}, bf16[384,384]{1,0:T(8,128)(2,1)S(1)}, u32[]{:S(2)}, u32[]{:S(2)}) collective-permute-start(bf16[384,384]{1,0:T(8,128)(2,1)} %get-tuple-element.155), channel_id=1, source_target_pairs={{0,1},{1,0},{2,3},{3,2},{4,5},{5,4},{6,7},{7,6},{8,9},{9,8},{10,11... | collective-permute-start | bytes 884744 | tf_op jit(solution)/shard_map/ppermute | solution.py:541
  9.4 10.9 %collective-permute-start.2 = (f32[2,2166]{1,0:T(2,128)}, f32[2,2166]{1,0:T(2,128)}, u32[]{:S(2)}, u32[]{:S(2)}) collective-permute-start(f32[2,2166]{1,0:T(2,128)} %constant_dynamic-update-slice_fusion), channel_id=1, source_target_pairs={{0,1},{1,0},{2,3},{3,2},{4,5},{5,4},{6,7},{7,6},{8,9},{9,8},{10,11... | collective-permute-start | bytes 51992 | tf_op jit(solution)/shard_map/ppermute | solution.py:541
  10.7 19.2 %collective-permute-start.3 = (bf16[768,384]{1,0:T(8,128)(2,1)}, bf16[768,384]{1,0:T(8,128)(2,1)}, u32[]{:S(2)}, u32[]{:S(2)}) collective-permute-start(bf16[768,384]{1,0:T(8,128)(2,1)} %get-tuple-element.147), channel_id=1, source_target_pairs={{0,1},{1,0},{2,3},{3,2},{4,5},{5,4},{6,7},{7,6},{8,9},{9,8},{10,11... | collective-permute-start | bytes 1769480 | tf_op jit(solution)/shard_map/ppermute | solution.py:541
  12.7 35.5 %collective-permute-start.6 = (bf16[384,384]{1,0:T(8,128)(2,1)}, bf16[384,384]{1,0:T(8,128)(2,1)}, u32[]{:S(2)}, u32[]{:S(2)}) collective-permute-start(bf16[384,384]{1,0:T(8,128)(2,1)} %get-tuple-element.154), channel_id=1, source_target_pairs={{0,1},{1,0},{2,3},{3,2},{4,5},{5,4},{6,7},{7,6},{8,9},{9,8},{10,11... | collective-permute-start | bytes 884744 | tf_op jit(solution)/shard_map/ppermute | solution.py:541
  12.7 33.3 %collective-permute-start.8 = (bf16[768,384]{1,0:T(8,128)(2,1)}, bf16[768,384]{1,0:T(8,128)(2,1)}, u32[]{:S(2)}, u32[]{:S(2)}) collective-permute-start(bf16[768,384]{1,0:T(8,128)(2,1)} %get-tuple-element.146), channel_id=1, source_target_pairs={{0,1},{1,0},{2,3},{3,2},{4,5},{5,4},{6,7},{7,6},{8,9},{9,8},{10,11... | collective-permute-start | bytes 1769480 | tf_op jit(solution)/shard_map/ppermute | solution.py:541
  20.2 121.6 %collective-permute-start.11 = (bf16[3,28,384]{2,1,0:T(8,128)(2,1)}, bf16[3,28,384]{2,1,0:T(8,128)(2,1)}, u32[]{:S(2)}, u32[]{:S(2)}) collective-permute-start(bf16[3,28,384]{2,1,0:T(8,128)(2,1)} %slice_bitcast_fusion.13), channel_id=1, source_target_pairs={{0,1},{1,0},{2,3},{3,2},{4,5},{5,4},{6,7},{7,6},{8,9},{9,8},{10,11... | collective-permute-start | bytes 193544 | tf_op jit(solution)/shard_map/ppermute | solution.py:541
  29.8 46.1 %collective-permute-start.4 = (bf16[768,384]{1,0:T(8,128)(2,1)}, bf16[768,384]{1,0:T(8,128)(2,1)S(1)}, u32[]{:S(2)}, u32[]{:S(2)}) collective-permute-start(bf16[768,384]{1,0:T(8,128)(2,1)} %collective-permute-done.3.oa_ref.refs_9_), channel_id=1, source_target_pairs={{0,2},{2,0},{4,6},{6,4},{8,10},{10,8},{12,14},{14,12},{16,18},{18,... | collective-permute-start | bytes 1769480 | tf_op jit(solution)/shard_map/ppermute | solution.py:544
  30.0 18.7 %collective-permute-start.1 = (bf16[384,384]{1,0:T(8,128)(2,1)S(1)}, bf16[384,384]{1,0:T(8,128)(2,1)S(1)}, u32[]{:S(2)}, u32[]{:S(2)}) collective-permute-start(bf16[384,384]{1,0:T(8,128)(2,1)S(1)} %collective-permute-done.refs_5_.refs_8_), channel_id=1, source_target_pairs={{0,2},{2,0},{4,6},{6,4},{8,10},{10,8},{12,14},{14,12},{16,18},{18,... | collective-permute-start | bytes 884744 | tf_op jit(solution)/shard_map/ppermute | solution.py:544
  46.0 80.1 %collective-permute-start.9 = (bf16[768,384]{1,0:T(8,128)(2,1)}, bf16[768,384]{1,0:T(8,128)(2,1)S(1)}, u32[]{:S(2)}, u32[]{:S(2)}) collective-permute-start(bf16[768,384]{1,0:T(8,128)(2,1)} %collective-permute-done.8.oa_ref.refs_9_), channel_id=1, source_target_pairs={{0,2},{2,0},{4,6},{6,4},{8,10},{10,8},{12,14},{14,12},{16,18},{18,... | collective-permute-start | bytes 1769480 | tf_op jit(solution)/shard_map/ppermute | solution.py:544
  48.2 49.0 %collective-permute-start.7 = (bf16[384,384]{1,0:T(8,128)(2,1)}, bf16[384,384]{1,0:T(8,128)(2,1)S(1)}, u32[]{:S(2)}, u32[]{:S(2)}) collective-permute-start(bf16[384,384]{1,0:T(8,128)(2,1)} %collective-permute-done.6.refs_6_.refs_8_), channel_id=1, source_target_pairs={{0,2},{2,0},{4,6},{6,4},{8,10},{10,8},{12,14},{14,12},{16,18},{18,... | collective-permute-start | bytes 884744 | tf_op jit(solution)/shard_map/ppermute | solution.py:544
  255.9 19.7 %collective-permute-start.28 = (bf16[2,384,384]{2,1,0:T(8,128)(2,1)}, bf16[2,384,384]{2,1,0:T(8,128)(2,1)}, u32[]{:S(2)}, u32[]{:S(2)}) collective-permute-start(bf16[2,384,384]{2,1,0:T(8,128)(2,1)} %get-tuple-element.88), channel_id=1, source_target_pairs={{0,2},{2,0},{4,6},{6,4},{8,10},{10,8},{12,14},{14,12},{16,18},{18,... | collective-permute-start | bytes 1769480 | tf_op jit(solution)/shard_map/ppermute | solution.py:544
  259.6 11.5 %collective-permute-start.10 = (f32[4,3,8,384]{3,2,1,0:T(8,128)S(1)}, f32[4,3,8,384]{3,2,1,0:T(8,128)S(1)}, u32[]{:S(2)}, u32[]{:S(2)}) collective-permute-start(f32[4,3,8,384]{3,2,1,0:T(8,128)S(1)} %slice_bitcast_fusion.11), channel_id=1, source_target_pairs={{0,1},{1,0},{2,3},{3,2},{4,5},{5,4},{6,7},{7,6},{8,9},{9,8},{10,11... | collective-permute-start | bytes 442376 | tf_op jit(solution)/shard_map/ppermute | solution.py:541
  265.8 8.4 %collective-permute-start.18 = (f32[72,128]{1,0:T(8,128)}, f32[72,128]{1,0:T(8,128)}, u32[]{:S(2)}, u32[]{:S(2)}) collective-permute-start(f32[72,128]{1,0:T(8,128)} %add.192), channel_id=1, source_target_pairs={{0,16},{2,18},{4,20},{6,22},{8,24},{10,26},{12,28},{14,30},{16,0},... | collective-permute-start | bytes 110600 | tf_op jit(solution)/shard_map/ppermute | solution.py:544
  268.4 48.8 %collective-permute-start.46 = (bf16[2,768,384]{2,1,0:T(8,128)(2,1)}, bf16[2,768,384]{2,1,0:T(8,128)(2,1)S(1)}, u32[]{:S(2)}, u32[]{:S(2)}) collective-permute-start(bf16[2,768,384]{2,1,0:T(8,128)(2,1)} %get-tuple-element.92), channel_id=1, source_target_pairs={{0,2},{2,0},{4,6},{6,4},{8,10},{10,8},{12,14},{14,12},{16,18},{18,... | collective-permute-start | bytes 3538952 | tf_op jit(solution)/shard_map/ppermute | solution.py:544
  270.7 7.5 %collective-permute-start.19 = (bf16[2,384,384]{2,1,0:T(8,128)(2,1)}, bf16[2,384,384]{2,1,0:T(8,128)(2,1)}, u32[]{:S(2)}, u32[]{:S(2)}) collective-permute-start(bf16[2,384,384]{2,1,0:T(8,128)(2,1)} %get-tuple-element.86), channel_id=1, source_target_pairs={{0,2},{2,0},{4,6},{6,4},{8,10},{10,8},{12,14},{14,12},{16,18},{18,... | collective-permute-start | bytes 1769480 | tf_op jit(solution)/shard_map/ppermute | solution.py:544
  271.8 60.0 %collective-permute-start.37 = (bf16[2,768,384]{2,1,0:T(8,128)(2,1)}, bf16[2,768,384]{2,1,0:T(8,128)(2,1)S(1)}, u32[]{:S(2)}, u32[]{:S(2)}) collective-permute-start(bf16[2,768,384]{2,1,0:T(8,128)(2,1)} %get-tuple-element.90), channel_id=1, source_target_pairs={{0,2},{2,0},{4,6},{6,4},{8,10},{10,8},{12,14},{14,12},{16,18},{18,... | collective-permute-start | bytes 3538952 | tf_op jit(solution)/shard_map/ppermute | solution.py:544
  277.0 9.4 %collective-permute-start.29 = (bf16[384,384]{1,0:T(8,128)(2,1)S(1)}, bf16[384,384]{1,0:T(8,128)(2,1)S(1)}, u32[]{:S(2)}, u32[]{:S(2)}) collective-permute-start(bf16[384,384]{1,0:T(8,128)(2,1)S(1)} %slice_bitcast_fusion.4), channel_id=1, source_target_pairs={{0,1},{1,0},{2,3},{3,2},{4,5},{5,4},{6,7},{7,6},{8,9},{9,8},{10,11... | collective-permute-start | bytes 884744 | tf_op jit(solution)/shard_map/ppermute | solution.py:541
  288.1 8.4 %collective-permute-start.20 = (bf16[384,384]{1,0:T(8,128)(2,1)S(1)}, bf16[384,384]{1,0:T(8,128)(2,1)S(1)}, u32[]{:S(2)}, u32[]{:S(2)}) collective-permute-start(bf16[384,384]{1,0:T(8,128)(2,1)S(1)} %slice_bitcast_fusion.6), channel_id=1, source_target_pairs={{0,1},{1,0},{2,3},{3,2},{4,5},{5,4},{6,7},{7,6},{8,9},{9,8},{10,11... | collective-permute-start | bytes 884744 | tf_op jit(solution)/shard_map/ppermute | solution.py:541
  298.0 18.0 %collective-permute-start.21 = (bf16[192,384]{1,0:T(8,128)(2,1)}, bf16[192,384]{1,0:T(8,128)(2,1)}, u32[]{:S(2)}, u32[]{:S(2)}) collective-permute-start(bf16[192,384]{1,0:T(8,128)(2,1)} %constant_dynamic-slice_fusion.11), channel_id=1, source_target_pairs={{0,4},{2,6},{4,0},{6,2},{8,12},{10,14},{12,8},{14,10},{16,20},{18,... | collective-permute-start | bytes 442376 | tf_op jit(solution)/shard_map/ppermute | solution.py:544
  302.2 11.0 %collective-permute-start.33 = (bf16[48,384]{1,0:T(8,128)(2,1)}, bf16[48,384]{1,0:T(8,128)(2,1)}, u32[]{:S(2)}, u32[]{:S(2)}) collective-permute-start(bf16[48,384]{1,0:T(8,128)(2,1)} %add_convert_fusion.14), channel_id=1, source_target_pairs={{0,16},{2,18},{4,20},{6,22},{8,24},{10,26},{12,28},{14,30},{16,0},... | collective-permute-start | bytes 110600 | tf_op jit(solution)/shard_map/ppermute | solution.py:544
  314.0 14.7 %collective-permute-start.34 = (bf16[96,384]{1,0:T(8,128)(2,1)S(1)}, bf16[96,384]{1,0:T(8,128)(2,1)S(1)}, u32[]{:S(2)}, u32[]{:S(2)}) collective-permute-start(bf16[96,384]{1,0:T(8,128)(2,1)S(1)} %maximum_select_fusion.11), channel_id=1, source_target_pairs={{0,8},{2,10},{4,12},{6,14},{8,0},{10,2},{12,4},{14,6},{16,24},{18,... | collective-permute-start | bytes 221192 | tf_op jit(solution)/shard_map/ppermute | solution.py:544
  323.9 17.7 %collective-permute-start.47 = (bf16[768,384]{1,0:T(8,128)(2,1)S(1)}, bf16[768,384]{1,0:T(8,128)(2,1)S(1)}, u32[]{:S(2)}, u32[]{:S(2)}) collective-permute-start(bf16[768,384]{1,0:T(8,128)(2,1)S(1)} %slice_bitcast_fusion), channel_id=1, source_target_pairs={{0,1},{1,0},{2,3},{3,2},{4,5},{5,4},{6,7},{7,6},{8,9},{9,8},{10,11... | collective-permute-start | bytes 1769480 | tf_op jit(solution)/shard_map/ppermute | solution.py:541
  328.8 9.3 %collective-permute-start.35 = (bf16[192,384]{1,0:T(8,128)(2,1)S(1)}, bf16[192,384]{1,0:T(8,128)(2,1)S(1)}, u32[]{:S(2)}, u32[]{:S(2)}) collective-permute-start(bf16[192,384]{1,0:T(8,128)(2,1)S(1)} %maximum_select_fusion.7), channel_id=1, source_target_pairs={{0,4},{2,6},{4,0},{6,2},{8,12},{10,14},{12,8},{14,10},{16,20},{18,... | collective-permute-start | bytes 442376 | tf_op jit(solution)/shard_map/ppermute | solution.py:544
  337.5 13.9 %collective-permute-start.38 = (bf16[768,384]{1,0:T(8,128)(2,1)S(1)}, bf16[768,384]{1,0:T(8,128)(2,1)S(1)}, u32[]{:S(2)}, u32[]{:S(2)}) collective-permute-start(bf16[768,384]{1,0:T(8,128)(2,1)S(1)} %slice_bitcast_fusion.2), channel_id=1, source_target_pairs={{0,1},{1,0},{2,3},{3,2},{4,5},{5,4},{6,7},{7,6},{8,9},{9,8},{10,11... | collective-permute-start | bytes 1769480 | tf_op jit(solution)/shard_map/ppermute | solution.py:541
  341.5 37.6 %collective-permute-start.27 = (bf16[384,384]{1,0:T(8,128)(2,1)S(1)}, bf16[384,384]{1,0:T(8,128)(2,1)S(1)}, u32[]{:S(2)}, u32[]{:S(2)}) collective-permute-start(bf16[384,384]{1,0:T(8,128)(2,1)S(1)} %maximum_select_fusion.2), channel_id=1, source_target_pairs={{0,2},{2,0},{4,6},{6,4},{8,10},{10,8},{12,14},{14,12},{16,18},{18,... | collective-permute-start | bytes 884744 | tf_op jit(solution)/shard_map/ppermute | solution.py:544
  341.8 9.5 %collective-permute-start.48 = (bf16[384,384]{1,0:T(8,128)(2,1)S(1)}, bf16[384,384]{1,0:T(8,128)(2,1)S(1)}, u32[]{:S(2)}, u32[]{:S(2)}) collective-permute-start(bf16[384,384]{1,0:T(8,128)(2,1)S(1)} %constant_dynamic-slice_fusion.2), channel_id=1, source_target_pairs={{0,4},{2,6},{4,0},{6,2},{8,12},{10,14},{12,8},{14,10},{16,20},{18,... | collective-permute-start | bytes 884744 | tf_op jit(solution)/shard_map/ppermute | solution.py:544
  351.7 8.7 %collective-permute-start.39 = (bf16[384,384]{1,0:T(8,128)(2,1)S(1)}, bf16[384,384]{1,0:T(8,128)(2,1)S(1)}, u32[]{:S(2)}, u32[]{:S(2)}) collective-permute-start(bf16[384,384]{1,0:T(8,128)(2,1)S(1)} %constant_dynamic-slice_fusion.5), channel_id=1, source_target_pairs={{0,4},{2,6},{4,0},{6,2},{8,12},{10,14},{12,8},{14,10},{16,20},{18,... | collective-permute-start | bytes 884744 | tf_op jit(solution)/shard_map/ppermute | solution.py:544
  362.9 7.3 %collective-permute-start.51 = (bf16[96,384]{1,0:T(8,128)(2,1)S(1)}, bf16[96,384]{1,0:T(8,128)(2,1)S(1)}, u32[]{:S(2)}, u32[]{:S(2)}) collective-permute-start(bf16[96,384]{1,0:T(8,128)(2,1)S(1)} %add_convert_fusion.10), channel_id=1, source_target_pairs={{0,16},{2,18},{4,20},{6,22},{8,24},{10,26},{12,28},{14,30},{16,0},... | collective-permute-start | bytes 221192 | tf_op jit(solution)/shard_map/ppermute | solution.py:544
  372.2 7.1 %collective-permute-start.42 = (bf16[96,384]{1,0:T(8,128)(2,1)S(1)}, bf16[96,384]{1,0:T(8,128)(2,1)S(1)}, u32[]{:S(2)}, u32[]{:S(2)}) collective-permute-start(bf16[96,384]{1,0:T(8,128)(2,1)S(1)} %add_convert_fusion.11), channel_id=1, source_target_pairs={{0,16},{2,18},{4,20},{6,22},{8,24},{10,26},{12,28},{14,30},{16,0},... | collective-permute-start | bytes 221192 | tf_op jit(solution)/shard_map/ppermute | solution.py:544
  376.4 7.4 %collective-permute-start.53 = (bf16[384,384]{1,0:T(8,128)(2,1)S(1)}, bf16[384,384]{1,0:T(8,128)(2,1)S(1)}, u32[]{:S(2)}, u32[]{:S(2)}) collective-permute-start(bf16[384,384]{1,0:T(8,128)(2,1)S(1)} %maximum_select_fusion.5), channel_id=1, source_target_pairs={{0,4},{2,6},{4,0},{6,2},{8,12},{10,14},{12,8},{14,10},{16,20},{18,... | collective-permute-start | bytes 884744 | tf_op jit(solution)/shard_map/ppermute | solution.py:544
  384.0 10.2 %collective-permute-start.54 = (bf16[768,384]{1,0:T(8,128)(2,1)S(1)}, bf16[768,384]{1,0:T(8,128)(2,1)S(1)}, u32[]{:S(2)}, u32[]{:S(2)}) collective-permute-start(bf16[768,384]{1,0:T(8,128)(2,1)S(1)} %maximum_select_fusion.1), channel_id=1, source_target_pairs={{0,2},{2,0},{4,6},{6,4},{8,10},{10,8},{12,14},{14,12},{16,18},{18,... | collective-permute-start | bytes 1769480 | tf_op jit(solution)/shard_map/ppermute | solution.py:544
  384.6 9.3 %collective-permute-start.44 = (bf16[384,384]{1,0:T(8,128)(2,1)S(1)}, bf16[384,384]{1,0:T(8,128)(2,1)S(1)}, u32[]{:S(2)}, u32[]{:S(2)}) collective-permute-start(bf16[384,384]{1,0:T(8,128)(2,1)S(1)} %maximum_select_fusion.4), channel_id=1, source_target_pairs={{0,4},{2,6},{4,0},{6,2},{8,12},{10,14},{12,8},{14,10},{16,20},{18,... | collective-permute-start | bytes 884744 | tf_op jit(solution)/shard_map/ppermute | solution.py:544
  (53 other events, 366.6 us)

commit v2 on v0

v2 whole, which is shorter than its diff:
```python
from functools import partial

import jax
import jax.numpy as jnp
import numpy as np
from jax import lax
from jax.experimental import pallas as pl
from jax.experimental.pallas import tpu as pltpu
from jax.sharding import PartitionSpec as P

C = 384
WIN = 7
SHIFT = 3
HD = 32
EPS = 1e-05
NEG = -1000000000.0
SCALE = HD**-0.5
F32 = jnp.float32
BF = jnp.bfloat16
SEG = 8
WROWS = WIN * SEG
WPAD = 64


def nn(a, b):
    return lax.dot_general(a, b, (((1,), (0,)), ((), ())), preferred_element_type=F32)


def nt(a, b):
    return lax.dot_general(a, b, (((1,), (1,)), ((), ())), preferred_element_type=F32)


def tn(a, b):
    return lax.dot_general(a, b, (((0,), (0,)), ((), ())), preferred_element_type=F32)


def norm_stats(x):
    mean = jnp.mean(x, -1, keepdims=True)
    cent = x - mean
    var = jnp.mean(cent * cent, -1, keepdims=True)
    rinv = lax.rsqrt(var + EPS)
    return cent * rinv, rinv


def norm_back(dz, xhat, rinv, gain):
    d = dz * gain
    return rinv * (
        d - jnp.mean(d, -1, keepdims=True) - xhat * jnp.mean(d * xhat, -1, keepdims=True)
    )


def tile_row(r, k, across):
    return (((r // WIN) * across + k) * WIN + r % WIN) * SEG


def zero_rows(n):
    return jnp.zeros((n, C), F32)


def head_mask():
    row = lax.broadcasted_iota(jnp.int32, (6 * WPAD, 6 * HD), 0) // WPAD
    col = lax.broadcasted_iota(jnp.int32, (6 * WPAD, 6 * HD), 1) // HD
    return (row == col).astype(BF)


def spread(x, mask):
    return jnp.concatenate([x] * 6, axis=0) * mask


def fold(o):
    lane = lax.broadcasted_iota(jnp.int32, (WPAD, 128), 1)

    def of(h, a, b):
        return o[WPAD * h : WPAD * (h + 1), a:b]

    one = jnp.where(lane < 96, of(2, 0, 128), of(3, 0, 128))
    one = jnp.where(lane < 64, of(1, 0, 128), one)
    one = jnp.where(lane < 32, of(0, 0, 128), one)
    two = jnp.where(lane[:, :64] < 32, of(4, 128, 192), of(5, 128, 192))
    return jnp.concatenate([one, two], axis=1)


def rows_at(i, n):
    return pl.ds(pl.multiple_of(i * n, n), n)


def iota(shape, dim):
    return lax.broadcasted_iota(jnp.int32, shape, dim)


def exact(a, b, ca, cb):
    return lax.dot_general(
        a,
        b,
        (((ca,), (cb,)), ((), ())),
        precision=lax.Precision.HIGHEST,
        preferred_element_type=F32,
    )


def offset_rows():
    return (12 - iota((16, 169), 0) == iota((16, 169), 1) // 13).astype(F32)


def offset_cols():
    return (iota((96, 169), 0) % 16 == iota((96, 169), 1) % 13).astype(F32)


def column_pick(kx):
    r = iota((96, 6 * WPAD), 0)
    c = iota((96, 6 * WPAD), 1)
    qx = c % 8
    return ((r // 16 == c // WPAD) & (r % 16 == qx - kx + WIN - 1) & (qx < WIN)).astype(F32)


def table_to_map(t, pos_ref):
    pos_ref[...] = jnp.zeros_like(pos_ref)
    group = (iota((8, 6 * WPAD), 1) % WPAD) // 8
    for kx in range(WIN):
        h = exact(t, column_pick(kx), 1, 0)
        g = jnp.zeros((8, 6 * WPAD), F32)
        for j in range(WIN):
            g = jnp.where(group == j, h[6 - j : 14 - j], g)
        for i in range(3):
            pos_ref[i, pl.ds(kx, 8, stride=8), :] = g[:, 128 * i : 128 * (i + 1)]


def map_to_table(pos_ref):
    group = (iota((16, 6 * WPAD), 1) % WPAD) // 8
    total = jnp.zeros((16, 96), F32)
    for kx in range(WIN):
        r = jnp.concatenate([pos_ref[i, pl.ds(kx, 8, stride=8), :] for i in range(3)], axis=1)
        h = jnp.zeros((16, 6 * WPAD), F32)
        for j in range(WIN):
            parts = [r, jnp.zeros((2 + j, 6 * WPAD), F32)]
            if j < 6:
                parts = [jnp.zeros((6 - j, 6 * WPAD), F32)] + parts
            h = jnp.where(group == j, jnp.concatenate(parts, axis=0), h)
        total = total + exact(h, column_pick(kx), 1, 1)
    return total


def shift_in(tile, x_ref, rows, across):
    for r in range(rows):
        for k in range(across):
            a = tile(r + SHIFT, k)
            b = tile(r + SHIFT, (k + 1) % across)
            x_ref[pl.ds(tile_row(r, k, across), SEG), :] = jnp.concatenate(
                [a[SHIFT:WIN], b[:SHIFT], zero_rows(1)], axis=0
            )


def shift_out(tile, x_ref, rows, across):
    for r in range(rows):
        for k in range(across):
            a = tile(r - SHIFT, (k - 1) % across)
            b = tile(r - SHIFT, k)
            x_ref[pl.ds(tile_row(r, k, across), SEG), :] = jnp.concatenate(
                [a[WIN - SHIFT : WIN], b[: WIN - SHIFT], zero_rows(1)], axis=0
            )

SMALL = 32


def prep_kernel(
    rows, across, tab_ref, qvb_ref, fb1_ref, crop_ref, info_ref, small_ref, lq_ref, lk_ref, pos_ref, c_ref
):
    tp = info_ref[1]
    cols = across * WIN
    height = crop_ref.shape[2]
    small_ref[...] = jnp.zeros_like(small_ref)
    for layer in range(2):
        tab = tab_ref[:, layer, :]
        wide = jnp.concatenate([jnp.broadcast_to(tab[h : h + 1], (16, 169)) for h in range(6)])
        t = exact(offset_rows(), wide * offset_cols(), 1, 1)
        small_ref[layer, 0:16, 0:96] = t
        small_ref[layer, 16:17, :] = fb1_ref[layer : layer + 1, 0:C]
        small_ref[layer, 17:18, :] = fb1_ref[layer : layer + 1, C:]
        small_ref[layer, 18:20, 0:192] = qvb_ref[layer]
        table_to_map(t, pos_ref.at[layer])
    c_ref[...] = jnp.zeros_like(c_ref)
    c_ref[0:cols, 0:height] = crop_ref[:, 0, :].astype(F32)
    crops = c_ref[...].astype(BF)
    row = iota((32, 128), 0)
    lane = iota((32, 128), 1)
    for layer in range(2):
        shift = SHIFT if layer == 1 else 0
        src = rows * tp + row + shift
        src = jnp.where(src >= height, src - height, src)
        grid = nt((src == lane).astype(BF), crops).astype(BF)
        for wc in range(across):
            qx = iota((128, 128), 1) % 8
            col = qx + (WIN * wc + shift)
            col = jnp.where(col >= cols, col - cols, col)
            pick = ((col == iota((128, 128), 0)) & (qx < WIN)).astype(BF)
            lab = nn(grid, pick)
            if layer == 1:
                g = rows * tp + row
                zr = (g >= height - WIN).astype(F32) + (g >= height - SHIFT).astype(F32)
                here = lane % 8 + WIN * wc
                zc = (here >= cols - WIN).astype(F32) + (here >= cols - SHIFT).astype(F32)
                lab = lab * 9.0 + zr * 3.0 + zc
            real = (iota((1, 128), 1) % 8 < WIN) & (iota((1, 128), 1) % WPAD < WROWS)
            for wr in range(rows // WIN):
                w = wr * across + wc
                mine = row == (lane % WPAD) // 8 + WIN * wr
                line = jnp.sum(jnp.where(mine, lab, 0.0), 0, keepdims=True)
                line = jnp.where(real, line, -1.0)
                lq_ref[layer, w : w + 1, :] = line
                lk_ref[layer, w] = jnp.broadcast_to(line, (128, 128)).T[:WPAD]


def qkv_weight_of(half, j, layer, qkvw_ref, a_ref, b_ref):
    if half == 0:
        return qkvw_ref[layer, j]
    return jnp.concatenate([a_ref[96 * j : 96 * (j + 1)], b_ref[96 * j : 96 * (j + 1)]], axis=0)


def proj_weight_of(half, layer, projw_ref, a_ref, b_ref):
    if half == 0:
        return projw_ref[layer]
    return jnp.concatenate([a_ref[288:384], b_ref[288:384]], axis=0)


def norm_windows(layer, wins, x_ref, xn_ref, gain_ref, bias_ref):
    gain = gain_ref[layer, 0:1]
    bias = bias_ref[layer, 0:1]

    def four(i, carry):
        xhat, _ = norm_stats(x_ref[rows_at(i, 4 * WROWS), :])
        xn = xhat * gain + bias
        for n in range(4):
            part = jnp.concatenate(
                [xn[n * WROWS : (n + 1) * WROWS], zero_rows(WPAD - WROWS)], axis=0
            )
            xn_ref[rows_at(4 * i + n, WPAD), :] = part.astype(BF)
        return carry

    lax.fori_loop(0, wins // 4, four, 0)


def project_half(xn_ref, qkv_ref, weight, qb, vb):
    n = xn_ref.shape[0] // 2

    def part(i, carry):
        at = rows_at(i, n)
        xn = xn_ref[at, :]
        q = nt(xn, weight(0))
        k = nt(xn, weight(1))
        v = nt(xn, weight(2))
        qkv_ref[0, at, :] = ((q + qb) * SCALE).astype(BF)
        qkv_ref[1, at, :] = k.astype(BF)
        qkv_ref[2, at, :] = (v + vb).astype(BF)
        return carry

    lax.fori_loop(0, 2, part, 0)


def attend_forward(halves, wins, group, layer, lq_ref, lk_ref, mask_ref):
    def body(i, carry):
        units = [(i * group + u, h) for u in range(group) for h in halves]
        scores = []
        for w, (qkv_ref, _, _, _) in units:
            at = rows_at(w, WPAD)
            scores.append(nt(qkv_ref[1, at, :], spread(qkv_ref[0, at, :], mask_ref[...])))
        probs = []
        for (w, (_, pos, p_ref, _)), s in zip(units, scores):
            same = lk_ref[layer, w] == lq_ref[layer, pl.ds(w, 1), :]
            same = jnp.concatenate([same] * 3, axis=1)
            s = jnp.where(same, s + jnp.concatenate([pos[n] for n in range(3)], axis=1), NEG)
            e = jnp.exp(s - jnp.max(s, 0, keepdims=True))
            p = (e * (1.0 / jnp.sum(e, 0, keepdims=True))).astype(BF)
            p_ref[w] = p
            probs.append(p)
        for (w, (qkv_ref, _, _, mix_ref)), p in zip(units, probs):
            at = rows_at(w, WPAD)
            mix_ref[at, :] = fold(tn(p, qkv_ref[2, at, :])).astype(BF)
        return carry

    lax.fori_loop(0, wins // group, body, 0)


def add_branch(wins, mixes, weights, bias, x_ref, hid_ref):
    n = 8

    def part(i, carry):
        res = bias
        for m_ref, w in zip(mixes, weights):
            res = res + nn(m_ref[rows_at(i, n * WPAD), :], w)
        for k in range(n):
            to = rows_at(i * n + k, WROWS)
            hid_ref[to, :] = x_ref[to, :] + res[k * WPAD : k * WPAD + WROWS]
        return carry

    lax.fori_loop(0, wins // n, part, 0)


def attn_own_kernel(rows, across, *refs):
    (tok_ref, gain_ref, bias_ref, pb_ref, qvb_ref, qkvw_ref, projw_ref) = refs[:7]
    (pos_ref, lq_ref, lk_ref) = refs[7:10]
    (x_ref, xn_ref, hid_ref, qkv_ref, p_ref, mix_ref, mask_ref) = refs[10:]
    wins = (rows // WIN) * across
    for r in range(rows):
        row = tok_ref[r].astype(F32)
        for k in range(across):
            x_ref[pl.ds(tile_row(r, k, across), SEG), :] = jnp.concatenate(
                [row[WIN * k : WIN * (k + 1)], zero_rows(1)], axis=0
            )
    mask_ref[...] = head_mask()
    norm_windows(0, wins, x_ref, xn_ref, gain_ref, bias_ref)
    project_half(
        xn_ref, qkv_ref, lambda j: qkvw_ref[0, j], qvb_ref[0, 0:1], qvb_ref[0, 1:2]
    )
    attend_forward(
        [(qkv_ref, pos_ref.at[0], p_ref, mix_ref)], wins, 8, 0, lq_ref, lk_ref, mask_ref
    )
    add_branch(wins, [mix_ref], [projw_ref[0]], pb_ref[0:1], x_ref, hid_ref)


def attn_other_kernel(rows, across, *refs):
    (part_ref, xn_ref, small_ref, a_ref, b_ref, lq_ref, lk_ref, info_ref) = refs[:8]
    (hid_ref, qkv_ref, p_ref, mix_ref, mask_ref, pos_ref, t_ref) = refs[8:]
    wins = (rows // WIN) * across
    mask_ref[...] = head_mask()
    bias = other_small(small_ref, 0, info_ref[0], t_ref, pos_ref)
    project_half(
        xn_ref,
        qkv_ref,
        lambda j: qkv_weight_of(1, j, 0, None, a_ref, b_ref),
        bias[0:1],
        bias[1:2],
    )
    attend_forward([(qkv_ref, pos_ref, p_ref, mix_ref)], wins, 8, 0, lq_ref, lk_ref, mask_ref)
    add_branch(
        wins, [mix_ref], [proj_weight_of(1, 0, None, a_ref, b_ref)], 0.0, part_ref, hid_ref
    )


def other_small(small_ref, layer, par, t_ref, pos_ref):
    first = par == 0

    def swapped(v, n):
        return jnp.where(first, v, jnp.concatenate([v[:, n : 2 * n], v[:, :n]], axis=1))

    t = swapped(small_ref[layer, 0:16, 0:96], 48)
    table_to_map(t, pos_ref)
    return swapped(small_ref[layer, 18:20, 0:192], 96)


def attn_both_kernel(rows, across, *refs):
    (st_ref, halo_ref, gain_ref, bias_ref, pb_ref, qvb_ref, qkvw_ref, projw_ref) = refs[:8]
    (pos_ref, small_ref, a_ref, b_ref, lq_ref, lk_ref, info_ref) = refs[8:15]
    (x_ref, xn_ref, hid_ref, qkv0_ref, p0_ref, mix0_ref) = refs[15:21]
    (qkv1_ref, p1_ref, mix1_ref, mask_ref, pos1_ref, t_ref) = refs[21:]
    wins = (rows // WIN) * across

    def tile(r, k):
        if r < rows:
            return st_ref[pl.ds(tile_row(r, k, across), SEG), :]
        return halo_ref[k, r - rows]

    shift_in(tile, x_ref, rows, across)
    mask_ref[...] = head_mask()
    bias = other_small(small_ref, 1, info_ref[0], t_ref, pos1_ref)
    norm_windows(1, wins, x_ref, xn_ref, gain_ref, bias_ref)
    project_half(
        xn_ref, qkv0_ref, lambda j: qkvw_ref[1, j], qvb_ref[1, 0:1], qvb_ref[1, 1:2]
    )
    project_half(
        xn_ref,
        qkv1_ref,
        lambda j: qkv_weight_of(1, j, 1, None, a_ref, b_ref),
        bias[0:1],
        bias[1:2],
    )
    attend_forward(
        [(qkv0_ref, pos_ref.at[1], p0_ref, mix0_ref), (qkv1_ref, pos1_ref, p1_ref, mix1_ref)],
        wins,
        4,
        1,
        lq_ref,
        lk_ref,
        mask_ref,
    )
    add_branch(
        wins,
        [mix0_ref, mix1_ref],
        [projw_ref[1], proj_weight_of(1, 1, None, a_ref, b_ref)],
        pb_ref[1:2],
        x_ref,
        hid_ref,
    )


def up_weight(part, layer, base, f1_ref, a_ref, b_ref):
    if part == 0:
        return f1_ref[layer]
    return jnp.concatenate([a_ref[base : base + C], b_ref[base : base + C]], axis=1)


def down_weight(part, layer, base, f2_ref, a_ref, b_ref):
    if part == 0:
        return f2_ref[layer]
    return jnp.concatenate([a_ref[base + C : base + 2 * C], b_ref[base + C : base + 2 * C]], axis=0)


def up_biases(layer, par, fb1_ref, small_ref):
    own = fb1_ref[layer : layer + 1]
    one, two = small_ref[layer, 16:17], small_ref[layer, 17:18]
    first = par == 0
    return own, jnp.concatenate(
        [jnp.where(first, one, two), jnp.where(first, two, one)], axis=1
    )


def gelu_pair(u):
    phi = 0.5 + 0.5 * lax.erf(u * (2.0**-0.5))
    slope = phi + u * (jnp.exp(-0.5 * u * u) * (2.0 * np.pi) ** -0.5)
    return (u * phi).astype(BF), slope.astype(BF)


def mlp_fwd_kernel(
    layer, base, hid_ref, gain_ref, bias_ref, fb1_ref, small_ref, fb2_ref, f1_ref, f2_ref, a_ref,
    b_ref, info_ref, st_ref, act_ref, gp_ref
):
    h = hid_ref[...]
    xhat, _ = norm_stats(h)
    n2 = (xhat * gain_ref[layer, 1:2] + bias_ref[layer, 1:2]).astype(BF)
    biases = up_biases(layer, info_ref[0], fb1_ref, small_ref)
    ups = [
        nn(n2, up_weight(p, layer, base, f1_ref, a_ref, b_ref)) + biases[p] for p in range(2)
    ]
    acts = []
    for p in range(2):
        act, slope = gelu_pair(ups[p])
        acts.append(act)
        for z in range(2):
            act_ref[2 * p + z] = act[:, C * z : C * (z + 1)]
            gp_ref[2 * p + z] = slope[:, C * z : C * (z + 1)]
    down = nn(acts[0], down_weight(0, layer, base, f2_ref, a_ref, b_ref)) + nn(
        acts[1], down_weight(1, layer, base, f2_ref, a_ref, b_ref)
    )
    st_ref[...] = h + fb2_ref[layer : layer + 1] + down


def mlp_back_rows(
    layer, base, at, g, h, slopes, gain, bias, f1_ref, f2_ref, a_ref, b_ref, refs, carry
):
    (gh_ref, df_ref, n2_ref, du_ref) = refs
    (sb, sg, sf, s1) = carry
    df = g.astype(BF)
    df_ref[at, :] = df
    sf = sf + jnp.sum(df.astype(F32), 0, keepdims=True)
    grads = [nt(df, down_weight(p, layer, base, f2_ref, a_ref, b_ref)) for p in range(2)]
    new = []
    parts = []
    for p in range(2):
        du = [
            (grads[p][:, C * z : C * (z + 1)] * slopes(2 * p + z).astype(F32)).astype(BF)
            for z in range(2)
        ]
        for z in range(2):
            du_ref[2 * p + z, at, :] = du[z]
            new.append(s1[2 * p + z] + jnp.sum(du[z].astype(F32), 0, keepdims=True))
        parts.append(jnp.concatenate(du, axis=1))
    dz = nt(parts[0], up_weight(0, layer, base, f1_ref, a_ref, b_ref)) + nt(
        parts[1], up_weight(1, layer, base, f1_ref, a_ref, b_ref)
    )
    xhat, rinv = norm_stats(h)
    n2_ref[at, :] = (xhat * gain + bias).astype(BF)
    sg = sg + jnp.sum(dz * xhat, 0, keepdims=True)
    sb = sb + jnp.sum(dz, 0, keepdims=True)
    gh_ref[at, :] = g + norm_back(dz, xhat, rinv, gain)
    return sb, sg, sf, tuple(new)


def mlp_weight_grads(par, n2_ref, df_ref, du_ref, act_ref, keep_ref, send_ref):
    n2 = n2_ref[...]
    df = df_ref[...]
    for slot, ref in ((1, send_ref), (0, keep_ref)):
        for part in range(2):
            q = (par ^ slot) if part == 0 else 2 + slot
            ref[part, 0:C, :] = tn(n2, du_ref[q]).astype(BF)
            ref[part, C:, :] = tn(act_ref[q], df).astype(BF)


def mlp_sums(carry, fb1_ref, sh_ref):
    sb, sg, sf, s1 = carry
    for q in range(4):
        fb1_ref[q : q + 1] = s1[q]
    sh_ref[0:1] = sg
    sh_ref[1:2] = sb
    sh_ref[2:3] = sf


def zero_sums():
    z = jnp.zeros((1, C), F32)
    return z, z, z, (z,) * 4


def mlp_both_kernel(rows, across, base, *refs):
    (cot_ref, halo_ref, hid_ref, gain_ref, bias_ref, fb1b_ref, small_ref, fb2_ref) = refs[:8]
    (f1_ref, f2_ref, a_ref, b_ref, info_ref) = refs[8:13]
    (st_ref, gh_ref, keep_ref, send_ref, fb1_ref, sh_ref) = refs[13:19]
    (g_ref, df_ref, n2_ref, du_ref, act_ref) = refs[19:]
    layer = 1
    for r in range(rows):
        s = r + SHIFT
        row = (cot_ref[s] if s < rows else halo_ref[s - rows]).astype(F32)
        for k in range(across):
            a = WIN * k + SHIFT
            if k < across - 1:
                piece = [row[a : a + WIN]]
            else:
                piece = [row[a:], row[:SHIFT]]
            g_ref[pl.ds(tile_row(r, k, across), SEG), :] = jnp.concatenate(
                piece + [zero_rows(1)], axis=0
            )
    gain = gain_ref[layer, 1:2]
    bias = bias_ref[layer, 1:2]
    par = info_ref[0]
    biases = up_biases(layer, par, fb1b_ref, small_ref)
    n = hid_ref.shape[0] // 2

    def block(i, carry):
        at = rows_at(i, n)
        h = hid_ref[at, :]
        xhat, _ = norm_stats(h)
        n2 = (xhat * gain + bias).astype(BF)
        ups = [
            nn(n2, up_weight(p, layer, base, f1_ref, a_ref, b_ref)) + biases[p] for p in range(2)
        ]
        acts = []
        slopes = []
        for p in range(2):
            act, slope = gelu_pair(ups[p])
            acts.append(act)
            for z in range(2):
                act_ref[2 * p + z, at, :] = act[:, C * z : C * (z + 1)]
                slopes.append(slope[:, C * z : C * (z + 1)])
        down = nn(acts[0], down_weight(0, layer, base, f2_ref, a_ref, b_ref)) + nn(
            acts[1], down_weight(1, layer, base, f2_ref, a_ref, b_ref)
        )
        st_ref[at, :] = h + fb2_ref[layer : layer + 1] + down
        return mlp_back_rows(
            layer, base, at, g_ref[at, :], h, lambda q: slopes[q], gain, bias, f1_ref, f2_ref,
            a_ref, b_ref, (gh_ref, df_ref, n2_ref, du_ref), carry
        )

    mlp_sums(lax.fori_loop(0, 2, block, zero_sums()), fb1_ref, sh_ref)
    mlp_weight_grads(par, n2_ref, df_ref, du_ref, act_ref, keep_ref, send_ref)


def mlp_bwd_kernel(rows, across, base, n_dep, *refs):
    (gin_ref, halo_ref, hid_ref, act_ref, gp_ref, gain_ref, bias_ref) = refs[:7]
    (f1_ref, f2_ref, a_ref, b_ref, info_ref) = refs[7:12]
    refs = refs[12 + n_dep :]
    (gh_ref, keep_ref, send_ref, fb1_ref, sh_ref) = refs[:5]
    (g_ref, df_ref, n2_ref, du_ref) = refs[5:]
    layer = 0

    def tile(r, k):
        if r >= 0:
            return gin_ref[pl.ds(tile_row(r, k, across), SEG), :]
        return halo_ref[k, r + SHIFT]

    shift_out(tile, g_ref, rows, across)
    gain = gain_ref[layer, 1:2]
    bias = bias_ref[layer, 1:2]
    n = hid_ref.shape[0] // 2

    def block(i, carry):
        at = rows_at(i, n)
        return mlp_back_rows(
            layer, base, at, g_ref[at, :], hid_ref[at, :], lambda q: gp_ref[q, at, :], gain, bias,
            f1_ref, f2_ref, a_ref, b_ref, (gh_ref, df_ref, n2_ref, du_ref), carry
        )

    mlp_sums(lax.fori_loop(0, 2, block, zero_sums()), fb1_ref, sh_ref)
    mlp_weight_grads(info_ref[0], n2_ref, df_ref, du_ref, act_ref, keep_ref, send_ref)


def window_grads(wins, gh_ref, da_ref):
    def four(i, s):
        g = gh_ref[rows_at(i, 4 * WROWS), :]
        for n in range(4):
            part = jnp.concatenate(
                [g[n * WROWS : (n + 1) * WROWS], zero_rows(WPAD - WROWS)], axis=0
            ).astype(BF)
            da_ref[rows_at(4 * i + n, WPAD), :] = part
            s = s + jnp.sum(part.astype(F32), 0, keepdims=True)
        return s

    return lax.fori_loop(0, wins // 4, four, jnp.zeros((1, C), F32))


def attend_backward(halves, wins, group, mask_ref):
    def body(i, carry):
        units = [(i * group + u, h) for u in range(group) for h in halves]
        first = []
        for w, (qkv_ref, p_ref, do_ref, dqkv_ref, _) in units:
            at = rows_at(w, WPAD)
            do = spread(do_ref[at, :], mask_ref[...])
            first.append(nt(qkv_ref[2, at, :], do))
            dqkv_ref[2, at, :] = nn(p_ref[w], do).astype(BF)
        second = []
        for (w, (_, p_ref, _, _, acc_ref)), dp in zip(units, first):
            p = p_ref[w].astype(F32)
            ds = p * (dp - jnp.sum(p * dp, 0, keepdims=True))
            for n in range(3):
                acc_ref[n] += ds[:, 128 * n : 128 * (n + 1)]
            second.append(ds.astype(BF))
        for (w, (qkv_ref, _, _, dqkv_ref, _)), ds in zip(units, second):
            at = rows_at(w, WPAD)
            dqkv_ref[1, at, :] = nn(ds, spread(qkv_ref[0, at, :], mask_ref[...])).astype(BF)
            dqkv_ref[0, at, :] = fold(tn(ds, qkv_ref[1, at, :])).astype(BF)
        return carry

    lax.fori_loop(0, wins // group, body, 0)


def half_grads(half, par, xn_ref, da_ref, mix_ref, dqkv_ref, row_ref, give):
    def put(value, at):
        if half == 0:
            row_ref[...] = value
            one = row_ref[pl.ds(pl.multiple_of(par * 96, 96), 96), :]
            two = row_ref[pl.ds(pl.multiple_of((1 - par) * 96, 96), 96), :]
        else:
            one, two = value[:96], value[96:]
        give(at, one.astype(BF), two.astype(BF))

    xn = xn_ref[...]
    for j in range(3):
        grad = tn(dqkv_ref[j], xn)
        put(grad * SCALE if j == 0 else grad, 96 * j)
    put(tn(mix_ref[...], da_ref[...]), 288)


def normed_grads(layer, wins, dqkvs, weights, gh_ref, x_ref, gain_ref, gx_ref):
    gain = gain_ref[layer, 0:1]
    n = 8

    def part(i, carry):
        sg, sb, sq = carry
        at = rows_at(i, n * WPAD)
        dn = nn(dqkvs[0][0, at, :], weights[0](0)) + nn(dqkvs[1][0, at, :], weights[1](0))
        dn = dn * SCALE
        for half in range(2):
            for j in (1, 2):
                dn = dn + nn(dqkvs[half][j, at, :], weights[half](j))
        new = []
        for half in range(2):
            for m, j in enumerate((0, 2)):
                new.append(
                    sq[half * 2 + m] + jnp.sum(dqkvs[half][j, at, :].astype(F32), 0, keepdims=True)
                )
        d = jnp.concatenate([dn[k * WPAD : k * WPAD + WROWS] for k in range(n)], axis=0)
        to = rows_at(i, n * WROWS)
        xhat, rinv = norm_stats(x_ref[to, :])
        sg = sg + jnp.sum(d * xhat, 0, keepdims=True)
        sb = sb + jnp.sum(d, 0, keepdims=True)
        gx_ref[to, :] = gh_ref[to, :] + norm_back(d, xhat, rinv, gain)
        return sg, sb, tuple(new)

    z = jnp.zeros((1, C), F32)
    zq = jnp.zeros((1, 6 * HD), F32)
    return lax.fori_loop(0, wins // n, part, (z, z, (zq,) * 4))


def small_grads(par, sums, projb, fb1_ref, sh_ref, accs, sm_ref):
    sg, sb, sq = sums
    sm_ref[...] = jnp.zeros_like(sm_ref)
    tables = [map_to_table(a) for a in accs]
    for q in range(4):
        half, z = q // 2, q % 2
        sm_ref[q, 0:1] = sg
        sm_ref[q, 1:2] = sb
        sm_ref[q, 2:3] = projb
        sm_ref[q, 3:6] = sh_ref[...]
        sm_ref[q, 6:7] = fb1_ref[q : q + 1]
        sm_ref[q, 7:8, 0:96] = sq[2 * half][:, 96 * z : 96 * (z + 1)] * SCALE
        sm_ref[q, 7:8, 128:224] = sq[2 * half + 1][:, 96 * z : 96 * (z + 1)]
        sm_ref[q, 8:24, 0:48] = tables[half][:, 48 * z : 48 * (z + 1)]


def attn_bwd_kernel(rows, across, n_dep, *refs):
    (gh_ref, x_ref, xn_ref, gain_ref, qkvw_ref, projw_ref, a_ref, b_ref, info_ref) = refs[:9]
    (fb1_ref, sh_ref, qkv0_ref, p0_ref, mix0_ref, qkv1_ref, p1_ref, mix1_ref) = refs[9:17]
    refs = refs[17 + n_dep :]
    (gin_ref, keep_ref, send_ref) = refs[:3]
    (da_ref, do_ref, dqkv0_ref, dqkv1_ref, acc_ref, mask_ref, row_ref, sm_ref) = refs[3:]
    layer = 1
    par = info_ref[0]
    wins = (rows // WIN) * across
    mask_ref[...] = head_mask()
    acc_ref[...] = jnp.zeros_like(acc_ref)
    projb = window_grads(wins, gh_ref, da_ref)
    for half in range(2):
        do_ref[half] = nt(
            da_ref[...], proj_weight_of(half, layer, projw_ref, a_ref, b_ref)
        ).astype(BF)
    attend_backward(
        [
            (qkv0_ref, p0_ref, do_ref.at[0], dqkv0_ref, acc_ref.at[0]),
            (qkv1_ref, p1_ref, do_ref.at[1], dqkv1_ref, acc_ref.at[1]),
        ],
        wins,
        4,
        mask_ref,
    )
    for half, mix_ref, dqkv_ref in ((1, mix1_ref, dqkv1_ref), (0, mix0_ref, dqkv0_ref)):

        def give(at, one, two, half=half):
            keep_ref[half, at : at + 96, :] = one
            send_ref[half, at : at + 96, :] = two

        half_grads(half, par, xn_ref, da_ref, mix_ref, dqkv_ref, row_ref, give)
    weights = [
        lambda j, half=half: qkv_weight_of(half, j, layer, qkvw_ref, a_ref, b_ref)
        for half in range(2)
    ]
    sums = normed_grads(
        layer, wins, [dqkv0_ref, dqkv1_ref], weights, gh_ref, x_ref, gain_ref, gin_ref
    )
    small_grads(par, sums, projb, fb1_ref, sh_ref, [acc_ref.at[0], acc_ref.at[1]], sm_ref)
    keep_ref[0, C:, :] = sm_ref[par].astype(BF)
    send_ref[0, C:, :] = sm_ref[1 - par].astype(BF)
    keep_ref[1, C:, :] = sm_ref[2].astype(BF)
    send_ref[1, C:, :] = sm_ref[3].astype(BF)


def attn_bwd_other_kernel(rows, across, n_dep, *refs):
    (gh_ref, xn_ref, projw_ref, a_ref, b_ref, qkv_ref, p_ref, mix_ref) = refs[:8]
    refs = refs[8 + n_dep :]
    (da_ref, do_ref, dqkv_ref, acc_ref, pb_ref, keep_ref, send_ref) = refs[:7]
    (do1_ref, mask_ref) = refs[7:]
    wins = (rows // WIN) * across
    mask_ref[...] = head_mask()
    acc_ref[...] = jnp.zeros_like(acc_ref)
    pb_ref[...] = window_grads(wins, gh_ref, da_ref)
    da = da_ref[...]
    do1_ref[...] = nt(da, proj_weight_of(1, 0, projw_ref, a_ref, b_ref)).astype(BF)
    do_ref[...] = nt(da, proj_weight_of(0, 0, projw_ref, a_ref, b_ref)).astype(BF)
    attend_backward([(qkv_ref, p_ref, do1_ref, dqkv_ref, acc_ref)], wins, 8, mask_ref)

    def give(at, one, two):
        keep_ref[at : at + 96, :] = one
        send_ref[at : at + 96, :] = two

    half_grads(1, None, xn_ref, da_ref, mix_ref, dqkv_ref, None, give)


def attn_bwd_own_kernel(rows, across, n_dep, *refs):
    (gh_ref, x_ref, xn_ref, gain_ref, qkvw_ref, a_ref, b_ref, info_ref) = refs[:8]
    (fb1_ref, sh_ref, da_ref, do_ref, dqkv1_ref, acc1_ref, pb_ref) = refs[8:15]
    (qkv_ref, p_ref, mix_ref) = refs[15:18]
    refs = refs[18 + n_dep :]
    (out_ref, keep_ref, send_ref) = refs[:3]
    (dqkv_ref, acc_ref, gx_ref, mask_ref, row_ref, sm_ref) = refs[3:]
    par = info_ref[0]
    wins = (rows // WIN) * across
    mask_ref[...] = head_mask()
    acc_ref[...] = jnp.zeros_like(acc_ref)
    attend_backward([(qkv_ref, p_ref, do_ref, dqkv_ref, acc_ref)], wins, 8, mask_ref)

    def give(at, one, two):
        keep_ref[at : at + 96, :] = one
        send_ref[at : at + 96, :] = two

    half_grads(0, par, xn_ref, da_ref, mix_ref, dqkv_ref, row_ref, give)
    weights = [
        lambda j, half=half: qkv_weight_of(half, j, 0, qkvw_ref, a_ref, b_ref)
        for half in range(2)
    ]
    sums = normed_grads(
        0, wins, [dqkv_ref, dqkv1_ref], weights, gh_ref, x_ref, gain_ref, gx_ref
    )
    small_grads(par, sums, pb_ref[...], fb1_ref, sh_ref, [acc_ref, acc1_ref], sm_ref)
    keep_ref[C : C + SMALL, :] = sm_ref[par].astype(BF)
    send_ref[C : C + SMALL, :] = sm_ref[1 - par].astype(BF)
    keep_ref[C + SMALL :, :] = sm_ref[2].astype(BF)
    send_ref[C + SMALL :, :] = sm_ref[3].astype(BF)
    for r in range(rows):
        parts = [gx_ref[pl.ds(tile_row(r, k, across), SEG), :][:WIN] for k in range(across)]
        out_ref[r] = jnp.concatenate(parts, axis=0)


def out_kernel(rows, across, st_ref, halo_ref, o_ref):
    for r in range(rows):
        parts = []
        for k in range(across):
            if r >= SHIFT:
                t = st_ref[pl.ds(tile_row(r - SHIFT, k, across), SEG), :]
            else:
                t = halo_ref[k, r]
            parts.append(t[:WIN])
        last = parts[-1]
        parts = [last[WIN - SHIFT :]] + parts[:-1] + [last[: WIN - SHIFT]]
        o_ref[r] = jnp.concatenate(parts, axis=0).astype(BF)


def final_kernel(*refs):
    (c0_ref, c1_ref, m0_ref, m1_ref, a0_ref, a1_ref, info_ref) = refs[:7]
    (qkv_ref, proj_ref, f1_ref, f2_ref, gain_ref, bias_ref, pb_ref, fb2_ref) = refs[7:15]
    (qvb_ref, fb1_ref, tab_ref) = refs[15:]
    first = info_ref[0] == 0

    def pair(mine, theirs, a, b):
        x = mine[a:b, :].astype(F32)
        y = theirs[a:b, :].astype(F32)
        return jnp.where(first, x, y), jnp.where(first, y, x)

    for layer in range(2):
        if layer == 1:
            mlp, attn, base = (c0_ref, c1_ref), (c0_ref, c1_ref), 2 * C
        else:
            mlp, attn, base = (m0_ref, m1_ref), (a0_ref, a1_ref), 0
        x, y = pair(*mlp, 0, C)
        f1_ref[layer, :, 0:C] = x
        f1_ref[layer, :, C:] = y
        x, y = pair(*mlp, C, 2 * C)
        f2_ref[layer, 0:C, :] = x
        f2_ref[layer, C:, :] = y
        for j in range(4):
            x, y = pair(*attn, base + 96 * j, base + 96 * (j + 1))
            if j < 3:
                qkv_ref[layer, j, 0:96, :] = x
                qkv_ref[layer, j, 96:, :] = y
            else:
                proj_ref[layer, 0:96, :] = x
                proj_ref[layer, 96:, :] = y
        x, y = pair(*attn, base + C, base + C + SMALL)
        gain_ref[layer, 0:1] = x[0:1]
        gain_ref[layer, 1:2] = x[3:4]
        bias_ref[layer, 0:1] = x[1:2]
        bias_ref[layer, 1:2] = x[4:5]
        pb_ref[layer : layer + 1] = x[2:3]
        fb2_ref[layer : layer + 1] = x[5:6]
        fb1_ref[layer : layer + 1, 0:C] = x[6:7]
        fb1_ref[layer : layer + 1, C:] = y[6:7]
        for n in range(2):
            qvb_ref[layer, n : n + 1, 0:96] = x[7:8, 128 * n : 128 * n + 96]
            qvb_ref[layer, n : n + 1, 96:192] = y[7:8, 128 * n : 128 * n + 96]
        t = jnp.concatenate([x[8:24, 0:48], y[8:24, 0:48]], axis=1)
        wide = exact(t, offset_rows(), 0, 0) * offset_cols()
        for h in range(6):
            tab_ref[h, layer : layer + 1, :] = jnp.sum(
                wide[16 * h : 16 * (h + 1)], 0, keepdims=True
            )


SMEM = pl.BlockSpec(memory_space=pltpu.SMEM)
VMEM = pl.BlockSpec(memory_space=pltpu.VMEM)
ANY = pl.BlockSpec(memory_space=pl.ANY)


def call(kernel, name, us, limit, operands, outs, scratch=()):
    args = []
    specs = []
    for op in operands:
        args.append(op[0] if isinstance(op, tuple) else op)
        specs.append(op[1] if isinstance(op, tuple) else VMEM)
    shapes = [jax.ShapeDtypeStruct(s, d) for s, d in outs]
    return pl.pallas_call(
        kernel,
        name=name,
        in_specs=specs,
        out_specs=[VMEM for s in shapes],
        out_shape=shapes,
        scratch_shapes=[pltpu.VMEM(s, d) for s, d in scratch],
        cost_estimate=pl.CostEstimate(
            flops=int(us * 1e9), bytes_accessed=1000000, transcendentals=0
        ),
        compiler_params=pltpu.CompilerParams(vmem_limit_bytes=limit * 2**20),
    )(*args)


def on_device(n_win, *args):
    (
        tokens,
        crop_ids,
        cotangent,
        norm_gain,
        norm_bias,
        qkv_weight,
        qv_bias,
        proj_weight,
        proj_bias,
        fc1_weight,
        fc1_bias,
        fc2_weight,
        fc2_bias,
        pos_table,
    ) = args
    rows, cols = tokens.shape[1:3]
    across = cols // WIN
    wins = (rows // WIN) * across
    ntok = wins * WROWS
    npad = wins * WPAD
    win = lax.axis_index("win")
    tp = lax.axis_index("tp")
    par = win % 2
    info = (jnp.stack([par, tp]).astype(jnp.int32), SMEM)
    bits = n_win.bit_length() - 1

    def to_tp(x):
        return lax.ppermute(x, "tp", [(0, 1), (1, 0)])

    def to_win(x, bit):
        return lax.ppermute(x, "win", [(i, i ^ (1 << bit)) for i in range(n_win)])

    qkv_t = qkv_weight.transpose(0, 2, 3, 1)

    def attn_quarter(layer):
        q = lax.dynamic_slice(qkv_t[layer], (0, par * 96, 0), (3, 96, C)).reshape(288, C)
        return jnp.concatenate([q, lax.dynamic_slice(proj_weight[layer], (par * 96, 0), (96, C))])

    def mlp_quarter(layer):
        return jnp.concatenate(
            [
                lax.dynamic_slice(fc1_weight[layer], (0, par * C), (C, C)),
                lax.dynamic_slice(fc2_weight[layer], (par * C, 0), (C, C)),
            ]
        )

    a0 = to_tp(attn_quarter(0))
    small, lq, lk, pos = call(
        partial(prep_kernel, rows, across),
        "prep",
        4,
        8,
        (pos_table.transpose(2, 0, 1), qv_bias, fc1_bias, crop_ids.transpose(2, 0, 1), info),
        [
            ((2, 24, C), F32),
            ((2, wins, 128), F32),
            ((2, wins, WPAD, 128), F32),
            ((2, 3, WPAD, 128), F32),
        ],
        [((128, 128), F32)],
    )
    small_o = to_tp(small)
    m0 = to_tp(mlp_quarter(0))
    w1 = to_tp(jnp.concatenate([attn_quarter(1), mlp_quarter(1)]))
    a0s = to_win(a0, 0)
    m0s = to_win(m0, 0)
    w1s = to_win(w1, 0)
    cot_halo = to_tp(cotangent[0, :SHIFT])
    tiles = (rows // WIN, across, WIN, SEG, C)
    mask = ((6 * WPAD, 6 * HD), BF)
    half_outs = [((3, npad, 192), BF), ((wins, WPAD, 6 * WPAD), BF), ((npad, 192), BF)]
    tok_f = ((ntok, C), F32)

    x0, xn0, part, qkv00, p00, mix00 = call(
        partial(attn_own_kernel, rows, across),
        "attn_own_0",
        8,
        12,
        (tokens[0], norm_gain, norm_bias, proj_bias, qv_bias, qkv_t, proj_weight, pos, lq, lk),
        [tok_f, ((npad, C), BF), tok_f] + half_outs,
        [mask],
    )
    hid0, qkv01, p01, mix01 = call(
        partial(attn_other_kernel, rows, across),
        "attn_other_0",
        7,
        12,
        (part, xn0, small_o, a0, a0s, lq, lk, info),
        [tok_f] + half_outs,
        [mask, ((3, WPAD, 128), F32), ((16, 96), F32)],
    )
    st0, act0, gp0 = call(
        partial(mlp_fwd_kernel, 0, 0),
        "mlp_fwd_0",
        7,
        24,
        (hid0, norm_gain, norm_bias, fc1_bias, small_o, fc2_bias, fc1_weight, fc2_weight, m0, m0s, info),
        [tok_f, ((4, ntok, C), BF), ((4, ntok, C), BF)],
    )
    halo = to_tp(st0.reshape(tiles)[0, :, :SHIFT])
    x1, xn1, hid1, qkv10, p10, mix10, qkv11, p11, mix11 = call(
        partial(attn_both_kernel, rows, across),
        "attn_fwd_1",
        12,
        14,
        (st0, halo, norm_gain, norm_bias, proj_bias, qv_bias, qkv_t, proj_weight)
        + (pos, small_o, w1, w1s, lq, lk, info),
        [tok_f, ((npad, C), BF), tok_f] + half_outs + half_outs,
        [mask, ((3, WPAD, 128), F32), ((16, 96), F32)],
    )
    mlp_outs = [((2, 2 * C, C), BF), ((2, 2 * C, C), BF), ((4, C), F32), ((3, C), F32)]
    mlp_scratch = [tok_f, ((ntok, C), BF), ((ntok, C), BF), ((4, ntok, C), BF)]
    st1, gh1, keep_m1, send_m1, gfb1, gsh1 = call(
        partial(mlp_both_kernel, rows, across, C),
        "mlp_both_1",
        18,
        30,
        (cotangent[0], cot_halo, hid1, norm_gain, norm_bias, fc1_bias, small_o, fc2_bias)
        + (fc1_weight, fc2_weight, w1, w1s, info),
        [tok_f, tok_f] + mlp_outs,
        mlp_scratch + [((4, ntok, C), BF)],
    )

    def add(a, b):
        return (a.astype(F32) + b.astype(F32)).astype(BF)

    m1_got = to_win(send_m1, 0)
    gin1, keep_a1, send_a1 = call(
        partial(attn_bwd_kernel, rows, across, 0),
        "attn_bwd_1",
        15,
        16,
        (gh1, x1, xn1, norm_gain, qkv_t, proj_weight, w1, w1s, info)
        + (gfb1, gsh1, qkv10, p10, mix10, qkv11, p11, mix11),
        [tok_f, ((2, C + SMALL, C), BF), ((2, C + SMALL, C), BF)],
        [
            ((npad, C), BF),
            ((2, npad, 192), BF),
            ((3, npad, 192), BF),
            ((3, npad, 192), BF),
            ((2, 3, WPAD, 128), F32),
            mask,
            ((192, C), F32),
            ((4, SMALL, C), F32),
        ],
    )
    halo = to_tp(gin1.reshape(tiles)[-1, :, WIN - SHIFT :])
    m1_sum = add(keep_m1, m1_got)
    a1_sum = add(keep_a1, to_win(send_a1, 0))
    m1_t = to_tp(m1_sum[1])
    a1_t = to_tp(a1_sum[1])
    gh0, keep_m0, send_m0, gfb0, gsh0 = call(
        partial(mlp_bwd_kernel, rows, across, 0, 2),
        "mlp_bwd_0",
        11,
        24,
        (gin1, halo, hid0, act0, gp0, norm_gain, norm_bias, fc1_weight, fc2_weight, m0, m0s, info)
        + ((m1_sum, ANY), (a1_sum, ANY)),
        [tok_f] + mlp_outs,
        mlp_scratch,
    )

    def split(acc, bit):
        n = acc.shape[0] // 2
        b = (win >> bit) & 1
        return (
            lax.dynamic_slice_in_dim(acc, b * n, n),
            lax.dynamic_slice_in_dim(acc, (1 - b) * n, n),
        )

    def join(acc, got, bit):
        b = (win >> bit) & 1
        return jnp.where(b == 0, jnp.concatenate([acc, got]), jnp.concatenate([got, acc]))

    m0_got = to_win(send_m0, 0)
    c1 = jnp.concatenate([add(m1_sum[0], m1_t), add(a1_sum[0], a1_t)])
    m0_sum = add(keep_m0, m0_got)
    c1_mine, c1_away = split(c1, 1)
    c1_y = to_win(c1_away, 1)
    m0_t = to_tp(m0_sum[1])
    da, do, dqkv1, acc1, pb0, keep_o0, send_o0 = call(
        partial(attn_bwd_other_kernel, rows, across, 3),
        "attn_bwd_other_0",
        8,
        16,
        (gh0, xn0, proj_weight, a0, a0s, qkv01, p01, mix01)
        + ((c1_mine, ANY), (c1_away, ANY), (m0_sum, ANY)),
        [
            ((npad, C), BF),
            ((npad, 192), BF),
            ((3, npad, 192), BF),
            ((3, WPAD, 128), F32),
            ((1, C), F32),
            ((C, C), BF),
            ((C, C), BF),
        ],
        [((npad, 192), BF), mask],
    )
    c1 = add(c1_mine, c1_y)
    o0_sum = add(keep_o0, to_win(send_o0, 0))
    o0_t = to_tp(o0_sum)
    m0_acc = add(m0_sum[0], m0_t)
    m0_mine, m0_away = split(m0_acc, 1)
    m0_y = to_win(m0_away, 1)
    c1_mine, c1_away = split(c1, 2)
    c1_z = to_win(c1_away, 2)
    grad_tokens, keep_a0, send_a0 = call(
        partial(attn_bwd_own_kernel, rows, across, 4),
        "attn_bwd_own_0",
        10,
        16,
        (gh0, x0, xn0, norm_gain, qkv_t, a0, a0s, info)
        + (gfb0, gsh0, da, do, dqkv1, acc1, pb0, qkv00, p00, mix00)
        + ((o0_sum, ANY), (m0_away, ANY), (m0_mine, ANY), (c1_away, ANY)),
        [((rows, cols, C), F32), ((C + 2 * SMALL, C), BF), ((C + 2 * SMALL, C), BF)],
        [
            ((3, npad, 192), BF),
            ((3, WPAD, 128), F32),
            tok_f,
            mask,
            ((192, C), F32),
            ((4, SMALL, C), F32),
        ],
    )
    a0_sum = add(keep_a0, to_win(send_a0, 0))
    small_t = to_tp(a0_sum[C + SMALL :])
    acc = jnp.concatenate(
        [add(a0_sum[:C], o0_t), add(a0_sum[C : C + SMALL], small_t)]
    )
    m0_acc = add(m0_mine, m0_y)
    c1 = add(c1_mine, c1_z)
    mine, away = split(acc, 1)
    acc = add(mine, to_win(away, 1))
    for bit in range(2, bits):
        acc = add(acc, to_win(acc, bit))
        m0_acc = add(m0_acc, to_win(m0_acc, bit))
        if bit > 2:
            c1 = add(c1, to_win(c1, bit))
    m0_acc = join(m0_acc, to_win(m0_acc, 1), 1)
    acc = join(acc, to_win(acc, 1), 1)
    c1 = join(c1, to_win(c1, 2), 2)
    c1 = join(c1, to_win(c1, 1), 1)
    halo = to_tp(st1.reshape(tiles)[-1, :, WIN - SHIFT :])
    (layer_out,) = call(
        partial(out_kernel, rows, across), "layer_out", 2, 8, (st1, halo), [((rows, cols, C), BF)]
    )
    outs = call(
        final_kernel,
        "final",
        4,
        12,
        (c1, to_win(c1, 0), m0_acc, to_win(m0_acc, 0), acc, to_win(acc, 0), info),
        [
            ((2, 3, 192, C), F32),
            ((2, 192, C), F32),
            ((2, C, 2 * C), F32),
            ((2, 2 * C, C), F32),
            ((2, 2, C), F32),
            ((2, 2, C), F32),
            ((2, C), F32),
            ((2, C), F32),
            ((2, 2, 192), F32),
            ((2, 2 * C), F32),
            ((6, 2, 169), F32),
        ],
    )
    (g_qkv, g_proj, g_f1, g_f2, g_gain, g_bias, g_pb, g_fb2, g_qvb, g_fb1, g_tab) = outs
    return (
        layer_out[None],
        grad_tokens[None],
        g_gain,
        g_bias,
        g_qkv.transpose(0, 3, 1, 2),
        g_qvb,
        g_proj,
        g_pb,
        g_f1,
        g_fb1,
        g_f2,
        g_fb2,
        g_tab.transpose(1, 2, 0),
    )


def solution(mesh):
    return jax.shard_map(
        partial(on_device, mesh.shape["win"]),
        mesh=mesh,
        in_specs=(
            P("win", "tp", None, None),
            P("win", None, None),
            P("win", "tp", None, None),
            P(),
            P(),
            P(None, None, None, "tp"),
            P(None, None, "tp"),
            P(None, "tp", None),
            P(),
            P(None, None, "tp"),
            P(None, "tp"),
            P(None, "tp", None),
            P(),
            P(None, None, "tp"),
        ),
        out_specs=(
            P("win", "tp", None, None),
            P("win", "tp", None, None),
            P(),
            P(),
            P(None, None, None, "tp"),
            P(None, None, "tp"),
            P(None, "tp", None),
            P(),
            P(None, None, "tp"),
            P(None, "tp"),
            P(None, "tp", None),
            P(),
            P(None, None, "tp"),
        ),
        check_vma=False,
    )
```

time: 1150 us -> 244 us (0.21)
  waiting for transfers between devices: 520 us -> 83.1 us
  local copies, waits for them, and re-layouts: 270 us -> 26.7 us
  matrix products: 178 us -> 0 us
  blocking collectives: 100 us -> 0 us
  Pallas kernels: 0 us -> 81.8 us
  other arithmetic: 59.4 us -> 11.8 us
  starting transfers between devices: 0.84 us -> 34.9 us
  between operations: 16.6 us -> 2.06 us
    unnamed x23 -> x0, waiting for transfers between devices: 281 us -> none
    dot_general x40 -> x0, matrix products: 174 us -> none  [the longest x2 50.7 us: layer_forward(): jnp.dot(flat_two, fc1_w, preferred_element_type=jnp.float32) + fc1_b]
    all_gather x8 -> x0, waiting for transfers between devices: 168 us -> none  [the longest x4 77.7 us: gather_grad(): lax.all_gather(grad_rows.astype(jnp.bfloat16), 'tp', axis=1, tiled=True)[0]]
    psum x2 -> x0, blocking collectives: 100 us -> none  [the longest x1 62.2 us: on_device(): sharded_all = lax.psum(sharded_all, 'win')]
    ppermute x0 -> x37, waiting for transfers between devices: none -> 83.1 us  [the longest x13 42.3 us: to_tp(): return lax.ppermute(x, 'tp', [(0, 1), (1, 0)])]
    pallas_call x0 -> x12, Pallas kernels: none -> 81.8 us  [call(): pl.pallas_call(kernel, name=name, in_specs=specs, out_specs=[VMEM for s i...]
    psum x1 -> x0, waiting for transfers between devices: 71 us -> none  [on_device(): sharded_all = lax.psum(sharded_all, 'win')]
    convert_element_type x17 -> x0, local copies, waits for them, and re-layouts: 61.3 us -> none  [the longest x8 33.8 us: layer_forward(): mixed_low = mixed_heads.reshape(-1, local_cols).astype(jnp.bfloat16)]
  transfers between devices with their start and end apart: 16 -> 37, of which waited for: 15 -> 17; matrix products, arithmetic and copies ran while one was open for 11% -> 9% of each run, Pallas kernels for 0% -> 20%
where the time goes in v2:
time: 244 us; the launch traced here: 240 us
  waiting for transfers between devices  83.1 us (34%)
  Pallas kernels  81.8 us (34%)
  starting transfers between devices  34.9 us (14%)
  local copies, waits for them, and re-layouts  26.7 us (11%)
  other arithmetic  11.8 us (5%)
    pallas_call x12, Pallas kernels, call(): pl.pallas_call(kernel, name=name, in_specs=specs, out_specs=[VMEM for s i...  81.8 us
    ppermute x13, waiting for transfers between devices, to_tp(): return lax.ppermute(x, 'tp', [(0, 1), (1, 0)])  42.3 us
    ppermute x24, waiting for transfers between devices, to_win(): return lax.ppermute(x, 'win', [(i, i ^ 1 << bit) for i in range(n_win)])  40.8 us
    ppermute x24, starting transfers between devices, to_win(): return lax.ppermute(x, 'win', [(i, i ^ 1 << bit) for i in range(n_win)])  20.4 us
    unnamed x129, local copies, waits for them, and re-layouts  18.1 us
    ppermute x13, starting transfers between devices, to_tp(): return lax.ppermute(x, 'tp', [(0, 1), (1, 0)])  14.5 us
    convert_element_type x19, other arithmetic, add(): return (a.astype(F32) + b.astype(F32)).astype(BF)  9.22 us
  transfers between devices with their start and end apart: 37, of which 17 were waited for; matrix products, arithmetic and copies ran while one was open for 9% of the time, Pallas kernels for 20%

profile of v2, /device:TPU:0, one launch (start us, length us, event | category | flops | bytes accessed | tf_op | source)
XLA Modules:
  0.0 240.4 jit_solution(4578580465330699375)
XLA Ops:
  3.5 2.9 %prep.1 = (f32[2,24,384]{2,1,0:T(8,128)S(1)}, f32[2,16,128]{2,1,0:T(8,128)S(1)}, f32[2,16,64,128]{3,2,1,0:T(8,128)S(1)}, f32[2,3,64,128]{3,2,1,0:T(8,128)S(1)}) custom-call(f32[6,2,169]{2,1,0:T(2,128)S(1)} %bitcast.69, f32[2,2,192]{2,1,0:T(2,128)S(1)} %copy-done.28, f32[2,768]{1,0:T(2,128)S(1)} %copy-done.24, s32[28,1,56]{2,1,0:T(1,128)S(1)} %bitcast.68, ...), custom_call_target="tpu_custom_call" | custom-call | flops 4000000000 | bytes 1000000 | tf_op jit(solution)/shard_map/prep/pallas_call | solution.py:864
  7.4 2.9 %collective-permute-start.1 = (f32[2,24,384]{2,1,0:T(8,128)S(1)}, f32[2,24,384]{2,1,0:T(8,128)S(1)}, u32[]{:S(2)}, u32[]{:S(2)}) collective-permute-start(f32[2,24,384]{2,1,0:T(8,128)S(1)} %get-tuple-element.79), channel_id=1, source_target_pairs={{0,1},{1,0},{2,3},{3,2},{4,5},{5,4},{6,7},{7,6},{8,9},{9,8},{10,11... | collective-permute-start | bytes 221192 | tf_op jit(solution)/shard_map/ppermute | solution.py:907
  17.8 2.1 collective-permute-start.4
  21.0 3.5 %collective-permute-done.2.refs_3_.refs_5_ = bf16[384,384]{1,0:T(8,128)(2,1)S(1)} collective-permute-done((bf16[384,384]{1,0:T(8,128)(2,1)}, bf16[384,384]{1,0:T(8,128)(2,1)S(1)}, u32[]{:S(2)}, u32[]{:S(2)}) %collective-permute-start.2) | collective-permute-done | bytes 294944 | tf_op jit(solution)/shard_map/ppermute | solution.py:907
  24.5 5.5 %attn_own_0.1 = (f32[896,384]{1,0:T(8,128)S(1)}, bf16[1024,384]{1,0:T(8,128)(2,1)S(1)}, f32[896,384]{1,0:T(8,128)S(1)}, bf16[3,1024,192]{2,1,0:T(8,128)(2,1)S(1)...) custom-call(bf16[28,28,384]{2,1,0:T(8,128)(2,1)S(1)} %bitcast.67, f32[2,2,384]{2,1,0:T(2,128)S(1)} %copy-done.27, ...), custom_call_target="tpu_custom_call" | custom-call | flops 8000000000 | bytes 1000000 | tf_op jit(solution)/shard_map/attn_own_0/pallas_call | solution.py:864
  32.9 4.3 %collective-permute-done.4.a_ref.refs_9_ = bf16[768,384]{1,0:T(8,128)(2,1)S(1)} collective-permute-done((bf16[768,384]{1,0:T(8,128)(2,1)S(1)}, bf16[768,384]{1,0:T(8,128)(2,1)S(1)}, u32[]{:S(2)}, u32[]{:S(2)}) %collective-permute-start.4) | collective-permute-done | bytes 589856 | tf_op jit(solution)/shard_map/ppermute | solution.py:907
  37.2 5.2 %attn_other_0.1 = (f32[896,384]{1,0:T(8,128)S(1)}, bf16[3,1024,192]{2,1,0:T(8,128)(2,1)S(1)}, bf16[16,64,384]{2,1,0:T(8,128)(2,1)S(1)}, bf16[1024,192]{1,0:T(8,128)(2,1)S(1)}) custom-call(f32[896,384]{1,0:T(8,128)S(1)} %get-tuple-element.77.refs_0_, bf16[1024,384]{1,0:T(8,128)(2,1)S(1)} %get-tuple-element.78.refs_1_.refs_2_, ...), custom_call_target="tpu_custom_call" | custom-call | flops 7000000000 | bytes 1000000 | tf_op jit(solution)/shard_map/attn_other_0/pallas_call | solution.py:864
  45.2 9.4 %collective-permute-done.7.refs_10_.refs_6_ = bf16[1152,384]{1,0:T(8,128)(2,1)S(1)} collective-permute-done((bf16[1152,384]{1,0:T(8,128)(2,1)S(1)}, bf16[1152,384]{1,0:T(8,128)(2,1)S(1)}, u32[]{:S(2)}, u32[]{:S(2)}) %collective-permute-start.7) | collective-permute-done | bytes 884768 | tf_op jit(solution)/shard_map/ppermute | solution.py:907
  54.6 4.5 %mlp_fwd_0.1 = (f32[896,384]{1,0:T(8,128)S(1)}, bf16[4,896,384]{2,1,0:T(8,128)(2,1)S(1)}, bf16[4,896,384]{2,1,0:T(8,128)(2,1)S(1)}) custom-call(f32[896,384]{1,0:T(8,128)S(1)} %get-tuple-element.80.hid_ref.refs_2_, f32[2,2,384]{2,1,0:T(2,128)S(1)} %copy-done.27, f32[2,2,384]{2,1,0:T(2,128)S(1)} %copy-done.26, f32[2,768]{1,0:T(2,128)S(1)} %copy-done.25, ...), custom_call_target="tpu_custom_call" | custom-call | flops 7000000000 | bytes 1000000 | tf_op jit(solution)/shard_map/mlp_fwd_0/pallas_call | solution.py:864
  61.2 1.8 collective-permute-start
  63.0 4.5 %collective-permute-done.6.refs_1_ = f32[4,3,8,384]{3,2,1,0:T(8,128)S(1)} collective-permute-done((f32[4,3,8,384]{3,2,1,0:T(8,128)S(1)}, f32[4,3,8,384]{3,2,1,0:T(8,128)S(1)}, u32[]{:S(2)}, u32[]{:S(2)}) %collective-permute-start.6) | collective-permute-done | bytes 147488 | tf_op jit(solution)/shard_map/ppermute | solution.py:907
  67.5 9.8 %attn_fwd_1.1 = (f32[896,384]{1,0:T(8,128)S(1)}, bf16[1024,384]{1,0:T(8,128)(2,1)S(1)}, f32[896,384]{1,0:T(8,128)S(1)}, bf16[3,1024,192]{2,1,0:T(8,128)(2,1)S(1)...) custom-call(f32[896,384]{1,0:T(8,128)S(1)} %get-tuple-element.81.ref, ...), custom_call_target="tpu_custom_call" | custom-call | flops 12000000000 | bytes 1000000 | tf_op jit(solution)/shard_map/attn_fwd_1/pallas_call | solution.py:864
  77.4 11.7 %mlp_both_1.1 = (f32[896,384]{1,0:T(8,128)S(1)}, f32[896,384]{1,0:T(8,128)S(1)}, bf16[2,768,384]{2,1,0:T(8,128)(2,1)S(1)}, bf16[2,768,384]{2,1,0:T(8,128)(2,1)},...) custom-call(bf16[28,28,384]{2,1,0:T(8,128)(2,1)S(1)} %bitcast.66, bf16[3,28,384]{2,1,0:T(8,128)(2,1)S(1)} %collective-permute-done.refs_1_, ...), custom_call_target="tpu_custom_call" | custom-call | flops 17999998976 | bytes 1000000 | tf_op jit(solution)/shard_map/mlp_both_1/pallas_call | solution.py:864
  89.1 14.3 %attn_bwd_1.1 = (f32[896,384]{1,0:T(8,128)S(1)}, bf16[2,416,384]{2,1,0:T(8,128)(2,1)S(1)}, bf16[2,416,384]{2,1,0:T(8,128)(2,1)S(1)}) custom-call(f32[896,384]{1,0:T(8,128)S(1)} %get-tuple-element.84.refs_0_, f32[896,384]{1,0:T(8,128)S(1)} %get-tuple-element.85.refs_1_, bf16[1024,384]{1,0:T(8,128)(2,1)S(1)} %get-tuple-element.86.refs_2_, ...), custom_call_target="tpu_custom_call" | custom-call | flops 15000000512 | bytes 1000000 | tf_op jit(solution)/shard_map/attn_bwd_1/pallas_call | solution.py:864
  107.9 1.8 collective-permute-start.10
  109.7 7.7 %collective-permute-done.14 = bf16[416,384]{1,0:T(8,128)(2,1)} collective-permute-done((bf16[416,384]{1,0:T(8,128)(2,1)}, bf16[416,384]{1,0:T(8,128)(2,1)}, u32[]{:S(2)}, u32[]{:S(2)}) %collective-permute-start.14) | collective-permute-done | bytes 319520 | tf_op jit(solution)/shard_map/ppermute | solution.py:907
  124.7 7.9 %mlp_bwd_0.1 = (f32[896,384]{1,0:T(8,128)S(1)}, bf16[2,768,384]{2,1,0:T(8,128)(2,1)S(1)}, bf16[2,768,384]{2,1,0:T(8,128)(2,1)}, f32[4,384]{1,0:T(4,128)S(1)}, f32[3,384]{1,0:T(4,128)S(1)}) custom-call(f32[896,384]{1,0:T(8,128)S(1)} %copy-done.11, f32[4,3,8,384]{3,2,1,0:T(8,128)S(1)} %collective-permute-done.10.refs_1_, f32[896,384]{1,0:T(8,128)S(1)} %copy-done.41, ...), custom_call_target="tpu_custom_call" | custom-call | flops 11000000512 | bytes 1000000 | tf_op jit(solution)/shard_map/mlp_bwd_0/pallas_call | solution.py:864
  136.8 9.7 %collective-permute-done.18 = bf16[592,384]{1,0:T(8,128)(2,1)S(1)} collective-permute-done((bf16[592,384]{1,0:T(8,128)(2,1)S(1)}, bf16[592,384]{1,0:T(8,128)(2,1)S(1)}, u32[]{:S(2)}, u32[]{:S(2)}) %collective-permute-start.18) | collective-permute-done | bytes 454688 | tf_op jit(solution)/shard_map/ppermute | solution.py:910
  152.2 5.3 %attn_bwd_other_0.1 = (bf16[1024,384]{1,0:T(8,128)(2,1)S(1)}, bf16[1024,192]{1,0:T(8,128)(2,1)S(1)}, bf16[3,1024,192]{2,1,0:T(8,128)(2,1)S(1)}, f32[3,64,128]{2,...) custom-call(f32[896,384]{1,0:T(8,128)S(1)} %copy-done.43, ...), custom_call_target="tpu_custom_call" | custom-call | flops 8000000000 | bytes 1000000 | tf_op jit(solution)/shard_map/attn_bwd_other_0/pallas_call | solution.py:864
  157.5 6.8 %collective-permute-done.17 = bf16[768,384]{1,0:T(8,128)(2,1)S(1)} collective-permute-done((bf16[768,384]{1,0:T(8,128)(2,1)S(1)}, bf16[768,384]{1,0:T(8,128)(2,1)S(1)}, u32[]{:S(2)}, u32[]{:S(2)}) %collective-permute-start.17) | collective-permute-done | bytes 589856 | tf_op jit(solution)/shard_map/ppermute | solution.py:907
  164.6 2.7 %collective-permute-start.24 = (bf16[384,384]{1,0:T(8,128)(2,1)S(1)}, bf16[384,384]{1,0:T(8,128)(2,1)S(1)}, u32[]{:S(2)}, u32[]{:S(2)}) collective-permute-start(bf16[384,384]{1,0:T(8,128)(2,1)S(1)} %constant_dynamic-slice_fusion.2.refs_19_), channel_id=1, source_target_pairs={{0,4},{2,6},{4,0},{6,2},{8,12},{10,14},{12,8},{14,10},{16,20},{18,... | collective-permute-start | bytes 884744 | tf_op jit(solution)/shard_map/ppermute | solution.py:910
  168.0 2.5 %collective-permute-start.20 = (bf16[296,384]{1,0:T(8,128)(2,1)}, bf16[296,384]{1,0:T(8,128)(2,1)}, u32[]{:S(2)}, u32[]{:S(2)}) collective-permute-start(bf16[296,384]{1,0:T(8,128)(2,1)} %add_convert_fusion.11), channel_id=1, source_target_pairs={{0,16},{2,18},{4,20},{6,22},{8,24},{10,26},{12,28},{14,30},{16,0},... | collective-permute-start | bytes 681992 | tf_op jit(solution)/shard_map/ppermute | solution.py:910
  172.2 9.6 %attn_bwd_own_0.1 = (f32[28,28,384]{2,1,0:T(8,128)S(1)}, bf16[448,384]{1,0:T(8,128)(2,1)S(1)}, bf16[448,384]{1,0:T(8,128)(2,1)S(1)}) custom-call(f32[896,384]{1,0:T(8,128)S(1)} %copy-done.43, f32[896,384]{1,0:T(8,128)S(1)} %copy-done.47, bf16[1024,384]{1,0:T(8,128)(2,1)S(1)} %copy-done.49, f32[2,2,384]{2,1,0:T(2,128)S(1)} %copy-done.27, ...), custom_call_target="tpu_custom_call" | custom-call | flops 10000000000 | bytes 1000000 | tf_op jit(solution)/shard_map/attn_bwd_own_0/pallas_call | solution.py:864
  181.9 2.1 collective-permute-start.30
  189.1 2.7 %collective-permute-done.30 = bf16[384,384]{1,0:T(8,128)(2,1)S(1)} collective-permute-done((bf16[384,384]{1,0:T(8,128)(2,1)S(1)}, bf16[384,384]{1,0:T(8,128)(2,1)S(1)}, u32[]{:S(2)}, u32[]{:S(2)}) %collective-permute-start.30) | collective-permute-done | bytes 294944 | tf_op jit(solution)/shard_map/ppermute | solution.py:907
  194.8 4.2 %collective-permute-done.25 = bf16[384,384]{1,0:T(8,128)(2,1)S(1)} collective-permute-done((bf16[384,384]{1,0:T(8,128)(2,1)S(1)}, bf16[384,384]{1,0:T(8,128)(2,1)S(1)}, u32[]{:S(2)}, u32[]{:S(2)}) %collective-permute-start.25) | collective-permute-done | bytes 294944 | tf_op jit(solution)/shard_map/ppermute | solution.py:910
  199.1 2.5 %collective-permute-start.26 = (bf16[384,384]{1,0:T(8,128)(2,1)S(1)}, bf16[384,384]{1,0:T(8,128)(2,1)S(1)}, u32[]{:S(2)}, u32[]{:S(2)}) collective-permute-start(bf16[384,384]{1,0:T(8,128)(2,1)S(1)} %add_convert_fusion.7), channel_id=1, source_target_pairs={{0,16},{2,18},{4,20},{6,22},{8,24},{10,26},{12,28},{14,30},{16,0},... | collective-permute-start | bytes 884744 | tf_op jit(solution)/shard_map/ppermute | solution.py:910
  204.3 10.3 %collective-permute-done.26 = bf16[384,384]{1,0:T(8,128)(2,1)S(1)} collective-permute-done((bf16[384,384]{1,0:T(8,128)(2,1)S(1)}, bf16[384,384]{1,0:T(8,128)(2,1)S(1)}, u32[]{:S(2)}, u32[]{:S(2)}) %collective-permute-start.26) | collective-permute-done | bytes 294944 | tf_op jit(solution)/shard_map/ppermute | solution.py:910
  217.0 8.6 %collective-permute-done.34 = bf16[208,384]{1,0:T(8,128)(2,1)S(1)} collective-permute-done((bf16[208,384]{1,0:T(8,128)(2,1)S(1)}, bf16[208,384]{1,0:T(8,128)(2,1)S(1)}, u32[]{:S(2)}, u32[]{:S(2)}) %collective-permute-start.34) | collective-permute-done | bytes 159776 | tf_op jit(solution)/shard_map/ppermute | solution.py:910
  226.7 4.8 %collective-permute-done.35 = bf16[208,384]{1,0:T(8,128)(2,1)S(1)} collective-permute-done((bf16[208,384]{1,0:T(8,128)(2,1)S(1)}, bf16[208,384]{1,0:T(8,128)(2,1)S(1)}, u32[]{:S(2)}, u32[]{:S(2)}) %collective-permute-start.35) | collective-permute-done | bytes 159776 | tf_op jit(solution)/shard_map/ppermute | solution.py:910
  233.5 2.3 copy.27
  235.8 4.1 %final.1 = (f32[2,3,192,384]{3,2,1,0:T(8,128)}, f32[2,192,384]{2,1,0:T(8,128)}, f32[2,384,768]{2,1,0:T(8,128)}, f32[2,768,384]{2,1,0:T(8,128)}, f32[2,2,384]{2,1...) custom-call(bf16[1184,384]{1,0:T(8,128)(2,1)S(1)} %maximum_select_fu, ...), custom_call_target="tpu_custom_call" | custom-call | flops 4000000000 | bytes 1000000 | tf_op jit(solution)/shard_map/final/pallas_call | solution.py:864
  (231 shorter events, 60.3 us)
Async XLA Ops:
  7.4 29.7 %collective-permute-start.1 = (f32[2,24,384]{2,1,0:T(8,128)S(1)}, f32[2,24,384]{2,1,0:T(8,128)S(1)}, u32[]{:S(2)}, u32[]{:S(2)}) collective-permute-start(f32[2,24,384]{2,1,0:T(8,128)S(1)} %get-tuple-element.79), channel_id=1, source_target_pairs={{0,1},{1,0},{2,3},{3,2},{4,5},{5,4},{6,7},{7,6},{8,9},{9,8},{10,11... | collective-permute-start | bytes 221192 | tf_op jit(solution)/shard_map/ppermute | solution.py:907
  14.3 10.1 %collective-permute-start.2 = (bf16[384,384]{1,0:T(8,128)(2,1)}, bf16[384,384]{1,0:T(8,128)(2,1)S(1)}, u32[]{:S(2)}, u32[]{:S(2)}) collective-permute-start(bf16[384,384]{1,0:T(8,128)(2,1)} %pad_maximum_fusion.2), channel_id=1, source_target_pairs={{0,1},{1,0},{2,3},{3,2},{4,5},{5,4},{6,7},{7,6},{8,9},{9,8},{10,11... | collective-permute-start | bytes 884744 | tf_op jit(solution)/shard_map/ppermute | solution.py:907
  17.8 19.3 %collective-permute-start.4 = (bf16[768,384]{1,0:T(8,128)(2,1)S(1)}, bf16[768,384]{1,0:T(8,128)(2,1)S(1)}, u32[]{:S(2)}, u32[]{:S(2)}) collective-permute-start(bf16[768,384]{1,0:T(8,128)(2,1)S(1)} %pad_maximum_fusion.1), channel_id=1, source_target_pairs={{0,1},{1,0},{2,3},{3,2},{4,5},{5,4},{6,7},{7,6},{8,9},{9,8},{10,11... | collective-permute-start | bytes 1769480 | tf_op jit(solution)/shard_map/ppermute | solution.py:907
  20.2 34.4 %collective-permute-start.7 = (bf16[1152,384]{1,0:T(8,128)(2,1)S(1)}, bf16[1152,384]{1,0:T(8,128)(2,1)S(1)}, u32[]{:S(2)}, u32[]{:S(2)}) collective-permute-start(bf16[1152,384]{1,0:T(8,128)(2,1)S(1)} %pad_maximum_fusion), channel_id=1, source_target_pairs={{0,1},{1,0},{2,3},{3,2},{4,5},{5,4},{6,7},{7,6},{8,9},{9,8},{10,11... | collective-permute-start | bytes 2654216 | tf_op jit(solution)/shard_map/ppermute | solution.py:907
  24.5 12.7 %collective-permute-start.3 = (bf16[384,384]{1,0:T(8,128)(2,1)S(1)}, bf16[384,384]{1,0:T(8,128)(2,1)S(1)}, u32[]{:S(2)}, u32[]{:S(2)}) collective-permute-start(bf16[384,384]{1,0:T(8,128)(2,1)S(1)} %collective-permute-done.2.refs_3_.refs_5_), channel_id=1, source_target_pairs={{0,2},{2,0},{4,6},{6,4},{8,10},{10,8},{12,14},{14,12},{16,18},{18,... | collective-permute-start | bytes 884744 | tf_op jit(solution)/shard_map/ppermute | solution.py:910
  37.1 17.5 %collective-permute-start.5 = (bf16[768,384]{1,0:T(8,128)(2,1)S(1)}, bf16[768,384]{1,0:T(8,128)(2,1)S(1)}, u32[]{:S(2)}, u32[]{:S(2)}) collective-permute-start(bf16[768,384]{1,0:T(8,128)(2,1)S(1)} %collective-permute-done.4.a_ref.refs_9_), channel_id=1, source_target_pairs={{0,2},{2,0},{4,6},{6,4},{8,10},{10,8},{12,14},{14,12},{16,18},{18,... | collective-permute-start | bytes 1769480 | tf_op jit(solution)/shard_map/ppermute | solution.py:910
  54.6 12.9 %collective-permute-start.8 = (bf16[1152,384]{1,0:T(8,128)(2,1)S(1)}, bf16[1152,384]{1,0:T(8,128)(2,1)S(1)}, u32[]{:S(2)}, u32[]{:S(2)}) collective-permute-start(bf16[1152,384]{1,0:T(8,128)(2,1)S(1)} %collective-permute-done.7.refs_10_.refs_6_), channel_id=1, source_target_pairs={{0,2},{2,0},{4,6},{6,4},{8,10},{10,8},{12,14},{14,12},{16,18},{18,... | collective-permute-start | bytes 2654216 | tf_op jit(solution)/shard_map/ppermute | solution.py:910
  60.8 6.7 %collective-permute-start.6 = (f32[4,3,8,384]{3,2,1,0:T(8,128)S(1)}, f32[4,3,8,384]{3,2,1,0:T(8,128)S(1)}, u32[]{:S(2)}, u32[]{:S(2)}) collective-permute-start(f32[4,3,8,384]{3,2,1,0:T(8,128)S(1)} %slice_bitcast_fusion.8), channel_id=1, source_target_pairs={{0,1},{1,0},{2,3},{3,2},{4,5},{5,4},{6,7},{7,6},{8,9},{9,8},{10,11... | collective-permute-start | bytes 442376 | tf_op jit(solution)/shard_map/ppermute | solution.py:907
  61.2 16.2 %collective-permute-start = (bf16[3,28,384]{2,1,0:T(8,128)(2,1)S(1)}, bf16[3,28,384]{2,1,0:T(8,128)(2,1)S(1)}, u32[]{:S(2)}, u32[]{:S(2)}) collective-permute-start(bf16[3,28,384]{2,1,0:T(8,128)(2,1)S(1)} %slice_bitcast_fusion.9), channel_id=1, source_target_pairs={{0,1},{1,0},{2,3},{3,2},{4,5},{5,4},{6,7},{7,6},{8,9},{9,8},{10,11... | collective-permute-start | bytes 193544 | tf_op jit(solution)/shard_map/ppermute | solution.py:907
  103.6 15.0 %collective-permute-start.11 = (bf16[2,768,384]{2,1,0:T(8,128)(2,1)}, bf16[2,768,384]{2,1,0:T(8,128)(2,1)}, u32[]{:S(2)}, u32[]{:S(2)}) collective-permute-start(bf16[2,768,384]{2,1,0:T(8,128)(2,1)} %get-tuple-element.99), channel_id=1, source_target_pairs={{0,2},{2,0},{4,6},{6,4},{8,10},{10,8},{12,14},{14,12},{16,18},{18,... | collective-permute-start | bytes 3538952 | tf_op jit(solution)/shard_map/ppermute | solution.py:910
  106.7 10.7 %collective-permute-start.14 = (bf16[416,384]{1,0:T(8,128)(2,1)}, bf16[416,384]{1,0:T(8,128)(2,1)}, u32[]{:S(2)}, u32[]{:S(2)}) collective-permute-start(bf16[416,384]{1,0:T(8,128)(2,1)} %slice_bitcast_fusion.4), channel_id=1, source_target_pairs={{0,1},{1,0},{2,3},{3,2},{4,5},{5,4},{6,7},{7,6},{8,9},{9,8},{10,11... | collective-permute-start | bytes 958472 | tf_op jit(solution)/shard_map/ppermute | solution.py:907
  107.9 12.9 %collective-permute-start.10 = (f32[4,3,8,384]{3,2,1,0:T(8,128)S(1)}, f32[4,3,8,384]{3,2,1,0:T(8,128)S(1)}, u32[]{:S(2)}, u32[]{:S(2)}) collective-permute-start(f32[4,3,8,384]{3,2,1,0:T(8,128)S(1)} %slice_bitcast_fusion.6), channel_id=1, source_target_pairs={{0,1},{1,0},{2,3},{3,2},{4,5},{5,4},{6,7},{7,6},{8,9},{9,8},{10,11... | collective-permute-start | bytes 442376 | tf_op jit(solution)/shard_map/ppermute | solution.py:907
  120.5 13.8 %collective-permute-start.13 = (bf16[768,384]{1,0:T(8,128)(2,1)S(1)}, bf16[768,384]{1,0:T(8,128)(2,1)S(1)}, u32[]{:S(2)}, u32[]{:S(2)}) collective-permute-start(bf16[768,384]{1,0:T(8,128)(2,1)S(1)} %slice_bitcast_fusion.2), channel_id=1, source_target_pairs={{0,1},{1,0},{2,3},{3,2},{4,5},{5,4},{6,7},{7,6},{8,9},{9,8},{10,11... | collective-permute-start | bytes 1769480 | tf_op jit(solution)/shard_map/ppermute | solution.py:907
  132.7 16.1 %collective-permute-start.15 = (bf16[2,768,384]{2,1,0:T(8,128)(2,1)}, bf16[2,768,384]{2,1,0:T(8,128)(2,1)}, u32[]{:S(2)}, u32[]{:S(2)}) collective-permute-start(bf16[2,768,384]{2,1,0:T(8,128)(2,1)} %get-tuple-element.110), channel_id=1, source_target_pairs={{0,2},{2,0},{4,6},{6,4},{8,10},{10,8},{12,14},{14,12},{16,18},{18,... | collective-permute-start | bytes 3538952 | tf_op jit(solution)/shard_map/ppermute | solution.py:910
  135.3 11.3 %collective-permute-start.18 = (bf16[592,384]{1,0:T(8,128)(2,1)S(1)}, bf16[592,384]{1,0:T(8,128)(2,1)S(1)}, u32[]{:S(2)}, u32[]{:S(2)}) collective-permute-start(bf16[592,384]{1,0:T(8,128)(2,1)S(1)} %fusion.3.refs_9_), channel_id=1, source_target_pairs={{0,4},{2,6},{4,0},{6,2},{8,12},{10,14},{12,8},{14,10},{16,20},{18,... | collective-permute-start | bytes 1363976 | tf_op jit(solution)/shard_map/ppermute | solution.py:910
  147.1 20.2 %collective-permute-start.19 = (bf16[296,384]{1,0:T(8,128)(2,1)S(1)}, bf16[296,384]{1,0:T(8,128)(2,1)S(1)}, u32[]{:S(2)}, u32[]{:S(2)}) collective-permute-start(bf16[296,384]{1,0:T(8,128)(2,1)S(1)} %constant_dynamic-slice_fusion.refs_21_), channel_id=1, source_target_pairs={{0,8},{2,10},{4,12},{6,14},{8,0},{10,2},{12,4},{14,6},{16,24},{18,... | collective-permute-start | bytes 681992 | tf_op jit(solution)/shard_map/ppermute | solution.py:910
  150.6 13.8 %collective-permute-start.17 = (bf16[768,384]{1,0:T(8,128)(2,1)S(1)}, bf16[768,384]{1,0:T(8,128)(2,1)S(1)}, u32[]{:S(2)}, u32[]{:S(2)}) collective-permute-start(bf16[768,384]{1,0:T(8,128)(2,1)S(1)} %slice_bitcast_fusion), channel_id=1, source_target_pairs={{0,1},{1,0},{2,3},{3,2},{4,5},{5,4},{6,7},{7,6},{8,9},{9,8},{10,11... | collective-permute-start | bytes 1769480 | tf_op jit(solution)/shard_map/ppermute | solution.py:907
  157.5 13.1 %collective-permute-start.16 = (bf16[384,384]{1,0:T(8,128)(2,1)S(1)}, bf16[384,384]{1,0:T(8,128)(2,1)S(1)}, u32[]{:S(2)}, u32[]{:S(2)}) collective-permute-start(bf16[384,384]{1,0:T(8,128)(2,1)S(1)} %get-tuple-element.120), channel_id=1, source_target_pairs={{0,2},{2,0},{4,6},{6,4},{8,10},{10,8},{12,14},{14,12},{16,18},{18,... | collective-permute-start | bytes 884744 | tf_op jit(solution)/shard_map/ppermute | solution.py:910
  164.6 7.4 %collective-permute-start.24 = (bf16[384,384]{1,0:T(8,128)(2,1)S(1)}, bf16[384,384]{1,0:T(8,128)(2,1)S(1)}, u32[]{:S(2)}, u32[]{:S(2)}) collective-permute-start(bf16[384,384]{1,0:T(8,128)(2,1)S(1)} %constant_dynamic-slice_fusion.2.refs_19_), channel_id=1, source_target_pairs={{0,4},{2,6},{4,0},{6,2},{8,12},{10,14},{12,8},{14,10},{16,20},{18,... | collective-permute-start | bytes 884744 | tf_op jit(solution)/shard_map/ppermute | solution.py:910
  168.0 15.9 %collective-permute-start.20 = (bf16[296,384]{1,0:T(8,128)(2,1)}, bf16[296,384]{1,0:T(8,128)(2,1)}, u32[]{:S(2)}, u32[]{:S(2)}) collective-permute-start(bf16[296,384]{1,0:T(8,128)(2,1)} %add_convert_fusion.11), channel_id=1, source_target_pairs={{0,16},{2,18},{4,20},{6,22},{8,24},{10,26},{12,28},{14,30},{16,0},... | collective-permute-start | bytes 681992 | tf_op jit(solution)/shard_map/ppermute | solution.py:910
  181.9 9.9 %collective-permute-start.30 = (bf16[384,384]{1,0:T(8,128)(2,1)S(1)}, bf16[384,384]{1,0:T(8,128)(2,1)S(1)}, u32[]{:S(2)}, u32[]{:S(2)}) collective-permute-start(bf16[384,384]{1,0:T(8,128)(2,1)S(1)} %add_convert_fusion.9.refs_18_), channel_id=1, source_target_pairs={{0,1},{1,0},{2,3},{3,2},{4,5},{5,4},{6,7},{7,6},{8,9},{9,8},{10,11... | collective-permute-start | bytes 884744 | tf_op jit(solution)/shard_map/ppermute | solution.py:907
  185.0 16.6 %collective-permute-start.21 = (bf16[296,384]{1,0:T(8,128)(2,1)S(1)}, bf16[296,384]{1,0:T(8,128)(2,1)S(1)}, u32[]{:S(2)}, u32[]{:S(2)}) collective-permute-start(bf16[296,384]{1,0:T(8,128)(2,1)S(1)} %add_convert_fusion.10), channel_id=1, source_target_pairs={{0,8},{2,10},{4,12},{6,14},{8,0},{10,2},{12,4},{14,6},{16,24},{18,... | collective-permute-start | bytes 681992 | tf_op jit(solution)/shard_map/ppermute | solution.py:910
  185.6 13.4 %collective-permute-start.25 = (bf16[384,384]{1,0:T(8,128)(2,1)S(1)}, bf16[384,384]{1,0:T(8,128)(2,1)S(1)}, u32[]{:S(2)}, u32[]{:S(2)}) collective-permute-start(bf16[384,384]{1,0:T(8,128)(2,1)S(1)} %get-tuple-element.148), channel_id=1, source_target_pairs={{0,8},{2,10},{4,12},{6,14},{8,0},{10,2},{12,4},{14,6},{16,24},{18,... | collective-permute-start | bytes 884744 | tf_op jit(solution)/shard_map/ppermute | solution.py:910
  193.0 10.6 %collective-permute-start.32 = (bf16[208,384]{1,0:T(8,128)(2,1)S(1)}, bf16[208,384]{1,0:T(8,128)(2,1)S(1)}, u32[]{:S(2)}, u32[]{:S(2)}) collective-permute-start(bf16[208,384]{1,0:T(8,128)(2,1)S(1)} %fusion.5), channel_id=1, source_target_pairs={{0,4},{2,6},{4,0},{6,2},{8,12},{10,14},{12,8},{14,10},{16,20},{18,... | collective-permute-start | bytes 479240 | tf_op jit(solution)/shard_map/ppermute | solution.py:910
  199.1 15.6 %collective-permute-start.26 = (bf16[384,384]{1,0:T(8,128)(2,1)S(1)}, bf16[384,384]{1,0:T(8,128)(2,1)S(1)}, u32[]{:S(2)}, u32[]{:S(2)}) collective-permute-start(bf16[384,384]{1,0:T(8,128)(2,1)S(1)} %add_convert_fusion.7), channel_id=1, source_target_pairs={{0,16},{2,18},{4,20},{6,22},{8,24},{10,26},{12,28},{14,30},{16,0},... | collective-permute-start | bytes 884744 | tf_op jit(solution)/shard_map/ppermute | solution.py:910
  201.8 14.8 %collective-permute-start.22 = (bf16[592,384]{1,0:T(8,128)(2,1)S(1)}, bf16[592,384]{1,0:T(8,128)(2,1)S(1)}, u32[]{:S(2)}, u32[]{:S(2)}) collective-permute-start(bf16[592,384]{1,0:T(8,128)(2,1)S(1)} %maximum_select_fusion.2), channel_id=1, source_target_pairs={{0,4},{2,6},{4,0},{6,2},{8,12},{10,14},{12,8},{14,10},{16,20},{18,... | collective-permute-start | bytes 1363976 | tf_op jit(solution)/shard_map/ppermute | solution.py:910
  203.8 12.7 %collective-permute-start.33 = (bf16[208,384]{1,0:T(8,128)(2,1)S(1)}, bf16[208,384]{1,0:T(8,128)(2,1)S(1)}, u32[]{:S(2)}, u32[]{:S(2)}) collective-permute-start(bf16[208,384]{1,0:T(8,128)(2,1)S(1)} %add_convert_fusion.14), channel_id=1, source_target_pairs={{0,8},{2,10},{4,12},{6,14},{8,0},{10,2},{12,4},{14,6},{16,24},{18,... | collective-permute-start | bytes 479240 | tf_op jit(solution)/shard_map/ppermute | solution.py:910
  214.8 11.2 %collective-permute-start.27 = (bf16[384,384]{1,0:T(8,128)(2,1)S(1)}, bf16[384,384]{1,0:T(8,128)(2,1)S(1)}, u32[]{:S(2)}, u32[]{:S(2)}) collective-permute-start(bf16[384,384]{1,0:T(8,128)(2,1)S(1)} %add_convert_fusion.6), channel_id=1, source_target_pairs={{0,4},{2,6},{4,0},{6,2},{8,12},{10,14},{12,8},{14,10},{16,20},{18,... | collective-permute-start | bytes 884744 | tf_op jit(solution)/shard_map/ppermute | solution.py:910
  216.5 9.0 %collective-permute-start.34 = (bf16[208,384]{1,0:T(8,128)(2,1)S(1)}, bf16[208,384]{1,0:T(8,128)(2,1)S(1)}, u32[]{:S(2)}, u32[]{:S(2)}) collective-permute-start(bf16[208,384]{1,0:T(8,128)(2,1)S(1)} %add_convert_fusion.13), channel_id=1, source_target_pairs={{0,16},{2,18},{4,20},{6,22},{8,24},{10,26},{12,28},{14,30},{16,0},... | collective-permute-start | bytes 479240 | tf_op jit(solution)/shard_map/ppermute | solution.py:910
  216.9 18.9 %collective-permute-start.23 = (bf16[1184,384]{1,0:T(8,128)(2,1)S(1)}, bf16[1184,384]{1,0:T(8,128)(2,1)S(1)}, u32[]{:S(2)}, u32[]{:S(2)}) collective-permute-start(bf16[1184,384]{1,0:T(8,128)(2,1)S(1)} %maximum_select_fusion.refs_0_), channel_id=1, source_target_pairs={{0,2},{2,0},{4,6},{6,4},{8,10},{10,8},{12,14},{14,12},{16,18},{18,... | collective-permute-start | bytes 2727944 | tf_op jit(solution)/shard_map/ppermute | solution.py:910
  226.2 9.6 %collective-permute-start.28 = (bf16[768,384]{1,0:T(8,128)(2,1)S(1)}, bf16[768,384]{1,0:T(8,128)(2,1)S(1)}, u32[]{:S(2)}, u32[]{:S(2)}) collective-permute-start(bf16[768,384]{1,0:T(8,128)(2,1)S(1)} %maximum_select_fusion.1.refs_2_), channel_id=1, source_target_pairs={{0,2},{2,0},{4,6},{6,4},{8,10},{10,8},{12,14},{14,12},{16,18},{18,... | collective-permute-start | bytes 1769480 | tf_op jit(solution)/shard_map/ppermute | solution.py:910
  226.3 6.3 %collective-permute-start.9 = (f32[4,3,8,384]{3,2,1,0:T(8,128)S(1)}, f32[4,3,8,384]{3,2,1,0:T(8,128)S(1)}, u32[]{:S(2)}, u32[]{:S(2)}) collective-permute-start(f32[4,3,8,384]{3,2,1,0:T(8,128)S(1)} %slice_bitcast_fusion.7), channel_id=1, source_target_pairs={{0,1},{1,0},{2,3},{3,2},{4,5},{5,4},{6,7},{7,6},{8,9},{9,8},{10,11... | collective-permute-start | bytes 442376 | tf_op jit(solution)/shard_map/ppermute | solution.py:907
  (69 other events, 383.4 us)
